TPU v7x, 256 devices: a whole 4x4x8 slice. The times are simulated.
256 devices in a mesh: head: 8 (over z), seq: 32 (over x, y, core).
Axes of the slice: x: 4, y: 4, z: 8, core: 2. Of those that a mesh axis runs over, the one named last changes fastest.
Arguments:
- q_routed: bfloat16 [8, 32768, 128], P('head', 'seq'), may hold values from -8 to 8
- k_routed: bfloat16 [8, 32768, 128], P('head', 'seq'), may hold values from -8 to 8
- v_routed: bfloat16 [8, 32768, 128], P('head', 'seq'), may hold values from -6 to 6
- memberships: int32 [8, 32768, 1], P('head', 'seq'), may hold values from 0 to 31; in each aligned block of 1024 rows (0 to 1023, 1024 to 2047, ..., all dimensions but the last counted through in order) at most 128 rows name the same one
- q_local: bfloat16 [8, 32768, 128], P('head', 'seq'), may hold values from -8 to 8
- k_local: bfloat16 [8, 32768, 128], P('head', 'seq'), may hold values from -8 to 8
- v_local: bfloat16 [8, 32768, 128], P('head', 'seq'), may hold values from -6 to 6
Outputs:
- out_routed: bfloat16 [8, 32768, 128], P('head', 'seq')
- out_local: bfloat16 [8, 32768, 128], P('head', 'seq')
Inputs may be any that keep to these rules, and one draw needn't show every extreme that they name: `memberships`: in each head, the 1024 tokens of one sequence block name any one cluster at most 128 times, a bound that some block reaches.
All inputs are finite; a program needn't handle non-finite values.
Results may differ from a plain program's by a relative error of at most 0.0049.
Values may be sent and summed in bfloat16 or wider, within the bound.
No kernel may reach another device: no remote copies, remote signals or barrier semaphores. Data moves between devices by JAX's collectives and lax.ppermute only.
A program may use at most 64 MiB of HBM per device.

v0:
```python
import jax
import jax.numpy as jnp
from jax import lax
from jax.experimental import pallas as pl
from jax.experimental.pallas import tpu as pltpu
from jax.sharding import Mesh
from jax.sharding import PartitionSpec as P

CLUSTERS = 32
CAP = 128
TOK = 1024
D = 128
SEQ = ("seq_0", "seq_1", "seq_2")
LOG2E = 1.4426950408889634
EXP_SCALE = LOG2E * D**-0.5
NEVER = -1e30
EMPTY = 256.0
GROUP = 8
VMEM = pl.BlockSpec(memory_space=pltpu.VMEM)


def params():
    return pltpu.CompilerParams(vmem_limit_bytes=56 * 1024 * 1024)


def pack_kernel(ids_ref, q_ref, k_ref, v_ref, sent_ref, rank_ref):
    ids = ids_ref[...]
    member = (ids == lax.broadcasted_iota(jnp.int32, (CLUSTERS, TOK), 0)).astype(jnp.float32)
    member_b = member.astype(jnp.bfloat16)
    upto = (
        lax.broadcasted_iota(jnp.int32, (128, 128), 0)
        <= lax.broadcasted_iota(jnp.int32, (128, 128), 1)
    ).astype(jnp.bfloat16)
    count = jnp.zeros((CLUSTERS, 1), jnp.float32)
    ranks = []
    for first in range(0, TOK, 128):
        seen = count + jnp.dot(
            member_b[:, first : first + 128], upto, preferred_element_type=jnp.float32
        )
        ranks.append(
            jnp.sum(member[:, first : first + 128] * seen, axis=0, keepdims=True) - 1.0
        )
        count = seen[:, 127:128]
    rank = jnp.concatenate(ranks, axis=1)
    rank_ref[...] = jnp.broadcast_to(rank, rank_ref.shape)
    at_rank = (
        rank.astype(jnp.int32) == lax.broadcasted_iota(jnp.int32, (CAP, TOK), 0)
    ).astype(jnp.bfloat16)
    rows = jnp.concatenate([q_ref[...], k_ref[...], v_ref[...]], axis=1)
    slot = lax.broadcasted_iota(jnp.int32, (CAP, D), 0).astype(jnp.float32)
    for base in range(0, CLUSTERS, GROUP):
        place = jnp.concatenate(
            [at_rank * member_b[c : c + 1] for c in range(base, base + GROUP)], axis=0
        )
        placed = jnp.dot(place, rows, preferred_element_type=jnp.float32)
        for i in range(GROUP):
            c = base + i
            mine = placed[i * CAP : (i + 1) * CAP]
            sent_ref[c, 0:CAP] = mine[:, 0:D].astype(jnp.bfloat16)
            used = slot < jnp.broadcast_to(count[c : c + 1], (CAP, D))
            sent_ref[c, CAP : 2 * CAP] = jnp.where(used, mine[:, D : 2 * D], EMPTY).astype(
                jnp.bfloat16
            )
            sent_ref[c, 2 * CAP : 3 * CAP] = mine[:, 2 * D : 3 * D].astype(jnp.bfloat16)


def pack(ids, q, k, v):
    return pl.pallas_call(
        pack_kernel,
        out_shape=(
            jax.ShapeDtypeStruct((CLUSTERS, 3 * CAP, D), jnp.bfloat16),
            jax.ShapeDtypeStruct((8, TOK), jnp.float32),
        ),
        in_specs=[VMEM] * 4,
        out_specs=(VMEM, VMEM),
        compiler_params=params(),
        name="pack_slots",
    )(ids, q, k, v)


def attend(queries, keys, values, allowed_of):
    scores = []
    for piece, allowed in zip(keys, allowed_of):
        s = lax.dot_general(
            queries, piece, (((1,), (1,)), ((), ())), preferred_element_type=jnp.float32
        )
        scores.append(s if allowed is None else jnp.where(allowed, s, NEVER))
    top = jnp.max(scores[0], axis=1, keepdims=True)
    for s in scores[1:]:
        top = jnp.maximum(top, jnp.max(s, axis=1, keepdims=True))
    shift = top * EXP_SCALE
    total = None
    for s, piece in zip(scores, values):
        weight = jnp.exp2(s * EXP_SCALE - shift).astype(jnp.bfloat16)
        part = jnp.dot(weight, piece, preferred_element_type=jnp.float32)
        total = part if total is None else total + part
    mass = total[:, D : 2 * D]
    return (total[:, 0:D] / jnp.where(mass > 0.0, mass, 1.0)).astype(jnp.bfloat16)


def routed_kernel(got_ref, out_ref, key_ref, value_ref):
    blocks = got_ref.shape[0]
    first = jnp.zeros((1, D), jnp.float32)
    for s in reversed(range(blocks)):
        row = got_ref[s, CAP : CAP + 16].astype(jnp.float32)[0:1]
        first = jnp.where(row < 100.0, row, first)
    filler = jnp.broadcast_to(first, (CAP, D))
    for s in range(blocks):
        key = got_ref[s, CAP : 2 * CAP].astype(jnp.float32)
        used = key < 100.0
        key_ref[s * CAP : (s + 1) * CAP] = jnp.where(used, key, filler).astype(jnp.bfloat16)
        value_ref[s * CAP : (s + 1) * CAP, 0:D] = got_ref[s, 2 * CAP : 3 * CAP]
        value_ref[s * CAP : (s + 1) * CAP, D : 2 * D] = used.astype(jnp.float32).astype(
            jnp.bfloat16
        )
    size = 2 * CAP
    within = lax.broadcasted_iota(jnp.int32, (size, size), 1) <= lax.broadcasted_iota(
        jnp.int32, (size, size), 0
    )
    for i in range(blocks // 2):
        low = i * size
        queries = got_ref[2 * i : 2 * i + 2, 0:CAP].reshape(size, D)
        keys, values, masks = [], [], []
        if low > 0:
            keys.append(key_ref[0:low])
            values.append(value_ref[0:low])
            masks.append(None)
        keys.append(key_ref[low : low + size])
        values.append(value_ref[low : low + size])
        masks.append(within)
        out_ref[2 * i : 2 * i + 2] = attend(queries, keys, values, masks).reshape(2, CAP, D)


def routed(got):
    blocks = got.shape[0]
    slots = blocks * CAP
    return pl.pallas_call(
        routed_kernel,
        out_shape=jax.ShapeDtypeStruct((blocks, CAP, D), jnp.bfloat16),
        in_specs=[VMEM],
        out_specs=VMEM,
        scratch_shapes=[
            pltpu.VMEM((slots, D), jnp.bfloat16),
            pltpu.VMEM((slots, 2 * D), jnp.bfloat16),
        ],
        compiler_params=params(),
        cost_estimate=pl.CostEstimate(
            flops=2 * slots * slots * D * 2, bytes_accessed=4 * slots * D * 2, transcendentals=0
        ),
        name="cluster_attention",
    )(got)


def local_kernel(at_ref, q_ref, k_ref, v_ref, far_ref, near_ref, out_ref, key_ref, value_ref):
    at = at_ref[0]
    own = k_ref[0:16].astype(jnp.float32)[0:1]
    nearest = near_ref[0, 0:16].astype(jnp.float32)[0:1]
    for b, ref in enumerate((far_ref, near_ref)):
        there = at >= 2 - b
        start = jnp.where(at == 0, own, nearest)
        filler = jnp.broadcast_to(start, (TOK, D))
        rows = pl.ds(b * TOK, TOK)
        key_ref[rows] = jnp.where(there, ref[0].astype(jnp.float32), filler).astype(jnp.bfloat16)
        value_ref[rows, 0:D] = ref[1]
        value_ref[rows, D : 2 * D] = jnp.full((TOK, D), jnp.where(there, 1.0, 0.0)).astype(
            jnp.bfloat16
        )
    key_ref[2 * TOK : 3 * TOK] = k_ref[...]
    value_ref[2 * TOK : 3 * TOK, 0:D] = v_ref[...]
    value_ref[2 * TOK : 3 * TOK, D : 2 * D] = jnp.ones((TOK, D), jnp.bfloat16)
    size = 256
    column = lax.broadcasted_iota(jnp.int32, (size, size), 1)
    line = lax.broadcasted_iota(jnp.int32, (size, size), 0)
    for i in range(TOK // size):
        low = i * size
        high = low + 2 * TOK
        spans = ((low, low + size), (low + size, high), (high, high + size))
        out_ref[low : low + size] = attend(
            q_ref[low : low + size],
            [key_ref[a:b] for a, b in spans],
            [value_ref[a:b] for a, b in spans],
            (column > line, None, column <= line),
        )


def windowed(at, q, k, v, far, near):
    return pl.pallas_call(
        local_kernel,
        out_shape=jax.ShapeDtypeStruct((TOK, D), jnp.bfloat16),
        in_specs=[pl.BlockSpec(memory_space=pltpu.SMEM)] + [VMEM] * 5,
        out_specs=VMEM,
        scratch_shapes=[
            pltpu.VMEM((3 * TOK, D), jnp.bfloat16),
            pltpu.VMEM((3 * TOK, 2 * D), jnp.bfloat16),
        ],
        compiler_params=params(),
        cost_estimate=pl.CostEstimate(
            flops=TOK * 2304 * D * 4, bytes_accessed=8 * TOK * D * 2, transcendentals=0
        ),
        name="window_attention",
    )(at, q, k, v, far, near)


def slot_kernel(ids_ref, rank_ref, at_rank_ref, ids_col_ref):
    rank = jnp.broadcast_to(rank_ref[0:1], (D, TOK)).T
    lane = lax.broadcasted_iota(jnp.int32, (TOK, CAP), 1)
    at_rank_ref[...] = (rank.astype(jnp.int32) == lane).astype(jnp.bfloat16)
    ids = jnp.broadcast_to(ids_ref[...].astype(jnp.float32), (D, TOK)).T
    ids_col_ref[...] = ids.astype(jnp.bfloat16)


def slots(ids, rank):
    return pl.pallas_call(
        slot_kernel,
        out_shape=(
            jax.ShapeDtypeStruct((TOK, CAP), jnp.bfloat16),
            jax.ShapeDtypeStruct((TOK, CAP), jnp.bfloat16),
        ),
        in_specs=[VMEM] * 2,
        out_specs=(VMEM, VMEM),
        compiler_params=params(),
        name="slot_columns",
    )(ids, rank)


def unpack_kernel(at_rank_ref, ids_ref, back_ref, out_ref):
    rows = 256
    for low in range(0, TOK, rows):
        at_rank = at_rank_ref[low : low + rows]
        ids = ids_ref[low : low + rows]
        zero = jnp.zeros_like(at_rank)
        picks = [
            jnp.where(ids == jnp.asarray(c, jnp.bfloat16), at_rank, zero) for c in range(CLUSTERS)
        ]
        pick = jnp.concatenate(picks, axis=1)
        out_ref[low : low + rows] = jnp.dot(
            pick, back_ref[...], preferred_element_type=jnp.float32
        ).astype(jnp.bfloat16)


def unpack(at_rank, ids_col, back):
    return pl.pallas_call(
        unpack_kernel,
        out_shape=jax.ShapeDtypeStruct((TOK, D), jnp.bfloat16),
        in_specs=[VMEM] * 3,
        out_specs=VMEM,
        compiler_params=params(),
        name="unpack_slots",
    )(at_rank, ids_col, back)


def passed_along(value, steps):
    count = lax.axis_size(SEQ)
    return lax.ppermute(value, SEQ, [(s, s + steps) for s in range(count - steps)])


def local(q_routed, k_routed, v_routed, memberships, q_local, k_local, v_local):
    seq_index = lax.axis_index(SEQ)
    pair = jnp.concatenate([k_local, v_local], axis=0)
    far = passed_along(pair, 2)
    near = passed_along(pair, 1)
    ids = memberships.reshape(1, TOK)
    sent, rank = pack(ids, q_routed[0], k_routed[0], v_routed[0])
    got = lax.all_to_all(sent, SEQ, split_axis=0, concat_axis=0, tiled=True)
    at_rank, ids_col = slots(ids, rank)
    out_local = windowed(
        seq_index.astype(jnp.int32).reshape(1), q_local[0], k_local[0], v_local[0], far, near
    )
    mixed = routed(got)
    back = lax.all_to_all(mixed, SEQ, split_axis=0, concat_axis=0, tiled=True)
    out_routed = unpack(at_rank, ids_col, back.reshape(CLUSTERS * CAP, D))
    return (out_routed[None], out_local[None])


def solution(mesh):
    torus = Mesh(
        mesh.devices.reshape(mesh.shape["head"], 4, 4, 2), ("head", "seq_0", "seq_1", "seq_2")
    )
    spec = P("head", SEQ, None)
    return jax.shard_map(
        local,
        mesh=torus,
        in_specs=(spec,) * 7,
        out_specs=(spec, spec),
        check_vma=False,
    )
```

profile of v0, /device:TPU:35, one launch (start us, length us, event | category | flops | bytes accessed | tf_op | source)
XLA Modules:
  0.0 121.0 jit_solution(10304264860257083631)
XLA Ops:
  0.6 7.5 %pack_slots.1 = (bf16[32,384,128]{2,1,0:T(8,128)(2,1)}, f32[8,1024]{1,0:T(8,128)}) custom-call(s32[1,1024]{1,0:T(1,128)} %bitcast.18, bf16[1024,128]{1,0:T(8,128)(2,1)} %bitcast.12, bf16[1024,128]{1,0:T(8,128)(2,1)} %bitcast.13, bf16[1024,128]{1,0:T(8,128)(2,1)} %bitcast.14), custom_call_target="tpu_custom_call" | custom-call | tf_op jit(solution)/shard_map/pack_slots/pallas_call | solution.py:68
  8.1 45.7 %all_to_all.10.got_ref = bf16[32,384,128]{2,1,0:T(8,128)(2,1)} all-to-all(bf16[32,384,128]{2,1,0:T(8,128)(2,1)} %get-tuple-element.9), channel_id=1, replica_groups=mesh['head'=8,'seq_0'=4,'seq_1'=4,'seq_2'=2] {'seq_0','seq_1','seq_2'}, dimensions={0} | all-to-all | bytes 6291456 | tf_op jit(solution)/shard_map/all_to_all | solution.py:264
  53.8 0.0 copy-start.1
  53.8 0.0 copy-start.2
  53.8 17.4 %cluster_attention.1 = bf16[32,128,128]{2,1,0:T(8,128)(2,1)} custom-call(bf16[32,384,128]{2,1,0:T(8,128)(2,1)} %all_to_all.10.got_ref), custom_call_target="tpu_custom_call" | custom-call | flops 8589934592 | bytes 4194304 | tf_op jit(solution)/shard_map/cluster_attention/pallas_call | solution.py:137
  71.3 5.7 %all-to-all-start.1 = ((bf16[32,128,128]{2,1,0:T(8,128)(2,1)}), bf16[32,128,128]{2,1,0:T(8,128)(2,1)S(1)}, u32[]{:S(2)}, u32[]{:S(2)}) async-start(bf16[32,128,128]{2,1,0:T(8,128)(2,1)} %cluster_attention.1), calls=%async_computation.1 | async-start | bytes 2097152 | tf_op jit(solution)/shard_map/all_to_all | solution.py:270
  77.0 0.0 copy-done.1
  77.0 0.0 copy-done.2
  77.0 3.3 %collective-permute-start.1 = (bf16[2,1024,128]{2,1,0:T(8,128)(2,1)S(1)}, bf16[2,1024,128]{2,1,0:T(8,128)(2,1)S(1)}, u32[]{:S(2)}, u32[]{:S(2)}) collective-permute-start(bf16[2,1024,128]{2,1,0:T(8,128)(2,1)S(1)} %constant_dynamic-update-slice_fusion), channel_id=1, source_target_pairs={{0,1},{1,2},{2,3},{3,4},{4,5},{5,6},{6,7},{7,8},{8,9},{9,10},{10,1... | collective-permute-start | bytes 1572872 | tf_op jit(solution)/shard_map/ppermute | solution.py:254
  80.4 3.1 %collective-permute-start = (bf16[2,1024,128]{2,1,0:T(8,128)(2,1)S(1)}, bf16[2,1024,128]{2,1,0:T(8,128)(2,1)S(1)}, u32[]{:S(2)}, u32[]{:S(2)}) collective-permute-start(bf16[2,1024,128]{2,1,0:T(8,128)(2,1)S(1)} %constant_dynamic-update-slice_fusion), channel_id=1, source_target_pairs={{0,2},{1,3},{2,4},{3,5},{4,6},{5,7},{6,8},{7,9},{8,10},{9,11},{10,... | collective-permute-start | bytes 1572872 | tf_op jit(solution)/shard_map/ppermute | solution.py:254
  83.5 1.8 %slot_columns.1 = (bf16[1024,128]{1,0:T(8,128)(2,1)}, bf16[1024,128]{1,0:T(8,128)(2,1)}) custom-call(s32[1,1024]{1,0:T(1,128)} %bitcast.19, f32[8,1024]{1,0:T(8,128)} %get-tuple-element.6.rank_ref), custom_call_target="tpu_custom_call" | custom-call | tf_op jit(solution)/shard_map/slot_columns/pallas_call | solution.py:213
  85.3 14.3 %collective-permute-done.1.near_ref = bf16[2,1024,128]{2,1,0:T(8,128)(2,1)S(1)} collective-permute-done((bf16[2,1024,128]{2,1,0:T(8,128)(2,1)S(1)}, bf16[2,1024,128]{2,1,0:T(8,128)(2,1)S(1)}, u32[]{:S(2)}, u32[]{:S(2)}) %collective-permute-start.1) | collective-permute-done | bytes 524320 | tf_op jit(solution)/shard_map/ppermute | solution.py:254
  99.7 0.0 copy-start.3
  99.7 9.2 %collective-permute-done.far_ref = bf16[2,1024,128]{2,1,0:T(8,128)(2,1)S(1)} collective-permute-done((bf16[2,1024,128]{2,1,0:T(8,128)(2,1)S(1)}, bf16[2,1024,128]{2,1,0:T(8,128)(2,1)S(1)}, u32[]{:S(2)}, u32[]{:S(2)}) %collective-permute-start) | collective-permute-done | bytes 524320 | tf_op jit(solution)/shard_map/ppermute | solution.py:254
  108.8 0.0 copy-start.4
  108.8 0.0 copy-done.3
  108.8 0.8 copy-done.4
  109.6 6.0 %window_attention.1 = bf16[1024,128]{1,0:T(8,128)(2,1)} custom-call(s32[1]{0:T(128)} %bitcast.6.at_ref, bf16[1024,128]{1,0:T(8,128)(2,1)} %bitcast.20, bf16[1024,128]{1,0:T(8,128)(2,1)} %bitcast.16, bf16[1024,128]{1,0:T(8,128)(2,1)} %bitcast.17, bf16[2,1024,128]{2,1,0:T(8,128)(2,1)} %copy-done.4, bf16[2,1024,128]{2,1,0:T(8,128)(2,1)} %copy-done.3), custom_call_target="tpu_custom_call" | custom-call | flops 1207959552 | bytes 2097152 | tf_op jit(solution)/shard_map/window_attention/pallas_call | solution.py:187
  115.6 0.0 all-to-all-done.1
  115.6 0.0 copy-start
  115.6 1.0 copy-done
  116.6 4.4 %unpack_slots.1 = bf16[1024,128]{1,0:T(8,128)(2,1)} custom-call(bf16[1024,128]{1,0:T(8,128)(2,1)} %get-tuple-element.7.at_rank_ref, bf16[1024,128]{1,0:T(8,128)(2,1)} %get-tuple-element.8.ids_ref, bf16[4096,128]{1,0:T(8,128)(2,1)} %bitcast.11), custom_call_target="tpu_custom_call" | custom-call | tf_op jit(solution)/shard_map/unpack_slots/pallas_call | solution.py:242
  (2 shorter events, 0.1 us)
Async XLA Ops:
  53.8 23.1 %copy-start.1 = (bf16[1,1024,128]{2,1,0:T(8,128)(2,1)S(1)}, bf16[1,1024,128]{2,1,0:T(8,128)(2,1)}, u32[]{:S(2)}) copy-start(bf16[1,1024,128]{2,1,0:T(8,128)(2,1)} %param.12) | copy-start | bytes 786436
  53.8 23.2 %copy-start.2 = (bf16[1,1024,128]{2,1,0:T(8,128)(2,1)S(1)}, bf16[1,1024,128]{2,1,0:T(8,128)(2,1)}, u32[]{:S(2)}) copy-start(bf16[1,1024,128]{2,1,0:T(8,128)(2,1)} %param.13) | copy-start | bytes 786436
  71.3 44.3 %all-to-all-start.1 = ((bf16[32,128,128]{2,1,0:T(8,128)(2,1)}), bf16[32,128,128]{2,1,0:T(8,128)(2,1)S(1)}, u32[]{:S(2)}, u32[]{:S(2)}) async-start(bf16[32,128,128]{2,1,0:T(8,128)(2,1)} %cluster_attention.1), calls=%async_computation.1 | async-start | bytes 2097152 | tf_op jit(solution)/shard_map/all_to_all | solution.py:270
  77.0 22.6 %collective-permute-start.1 = (bf16[2,1024,128]{2,1,0:T(8,128)(2,1)S(1)}, bf16[2,1024,128]{2,1,0:T(8,128)(2,1)S(1)}, u32[]{:S(2)}, u32[]{:S(2)}) collective-permute-start(bf16[2,1024,128]{2,1,0:T(8,128)(2,1)S(1)} %constant_dynamic-update-slice_fusion), channel_id=1, source_target_pairs={{0,1},{1,2},{2,3},{3,4},{4,5},{5,6},{6,7},{7,8},{8,9},{9,10},{10,1... | collective-permute-start | bytes 1572872 | tf_op jit(solution)/shard_map/ppermute | solution.py:254
  80.4 28.4 %collective-permute-start = (bf16[2,1024,128]{2,1,0:T(8,128)(2,1)S(1)}, bf16[2,1024,128]{2,1,0:T(8,128)(2,1)S(1)}, u32[]{:S(2)}, u32[]{:S(2)}) collective-permute-start(bf16[2,1024,128]{2,1,0:T(8,128)(2,1)S(1)} %constant_dynamic-update-slice_fusion), channel_id=1, source_target_pairs={{0,2},{1,3},{2,4},{3,5},{4,6},{5,7},{6,8},{7,9},{8,10},{9,11},{10,... | collective-permute-start | bytes 1572872 | tf_op jit(solution)/shard_map/ppermute | solution.py:254
  99.7 9.2 %copy-start.3 = (bf16[2,1024,128]{2,1,0:T(8,128)(2,1)}, bf16[2,1024,128]{2,1,0:T(8,128)(2,1)S(1)}, u32[]{:S(2)}) copy-start(bf16[2,1024,128]{2,1,0:T(8,128)(2,1)S(1)} %collective-permute-done.1.near_ref) | copy-start | bytes 1572868
  108.8 0.8 copy-start.4
  115.6 1.0 copy-start
where the time goes:
time: 121 us
  blocking collectives  45.7 us (38%)
  Pallas kernels  37.1 us (31%)
  waiting for transfers between devices  23.5 us (19%)
  starting transfers between devices  12.1 us (10%)
  local copies, waits for them, and re-layouts  1.83 us (2%)
    all_to_all x1, blocking collectives, local(): got = lax.all_to_all(sent, SEQ, split_axis=0, concat_axis=0, tiled=True)  45.7 us
    ppermute x2, waiting for transfers between devices, passed_along(): lax.ppermute(value, SEQ, [(s, s + steps) for s in range(count - steps)])  23.5 us
    pallas_call x1, Pallas kernels, routed(): pl.pallas_call(routed_kernel, out_shape=jax.ShapeDtypeStruct((blocks, CAP...  17.4 us
    pallas_call x1, Pallas kernels, pack(): pl.pallas_call(pack_kernel, out_shape=(jax.ShapeDtypeStruct((CLUSTERS, 3...  7.51 us
    ppermute x2, starting transfers between devices, passed_along(): lax.ppermute(value, SEQ, [(s, s + steps) for s in range(count - steps)])  6.43 us
    pallas_call x1, Pallas kernels, windowed(): pl.pallas_call(local_kernel, out_shape=jax.ShapeDtypeStruct((TOK, D), jnp...  5.96 us
    all_to_all x1, starting transfers between devices, local(): back = lax.all_to_all(mixed, SEQ, split_axis=0, concat_axis=0, tiled=True)  5.69 us
    pallas_call x1, Pallas kernels, unpack(): pl.pallas_call(unpack_kernel, out_shape=jax.ShapeDtypeStruct((TOK, D), jn...  4.43 us
  transfers between devices with their start and end apart: 3, of which 2 were waited for; matrix products, arithmetic and copies ran while one was open for 0% of the time, Pallas kernels for 6%

commit v1 on v0

--- a/solution.py
+++ b/solution.py
@@ -266,6 +266,7 @@
     out_local = windowed(
         seq_index.astype(jnp.int32).reshape(1), q_local[0], k_local[0], v_local[0], far, near
     )
+    got, out_local = lax.optimization_barrier((got, out_local))
     mixed = routed(got)
     back = lax.all_to_all(mixed, SEQ, split_axis=0, concat_axis=0, tiled=True)
     out_routed = unpack(at_rank, ids_col, back.reshape(CLUSTERS * CAP, D))

time: 121 us -> 124 us (1.025)
  the two profiles are of different devices: /device:TPU:35 before, /device:TPU:1 now
where the time goes in v1:
time: 124 us; the launch traced here: 123 us
  waiting for transfers between devices  57.2 us (46%)
  Pallas kernels  37 us (30%)
  starting transfers between devices  23.6 us (19%)
  local copies, waits for them, and re-layouts  5 us (4%)
    ppermute x2, waiting for transfers between devices, passed_along(): lax.ppermute(value, SEQ, [(s, s + steps) for s in range(count - steps)])  42.1 us
    pallas_call x1, Pallas kernels, routed(): pl.pallas_call(routed_kernel, out_shape=jax.ShapeDtypeStruct((blocks, CAP...  17.4 us
    all_to_all x1, waiting for transfers between devices, local(): back = lax.all_to_all(mixed, SEQ, split_axis=0, concat_axis=0, tiled=True)  15.1 us
    all_to_all x1, starting transfers between devices, local(): got = lax.all_to_all(sent, SEQ, split_axis=0, concat_axis=0, tiled=True)  8.72 us
    pallas_call x1, Pallas kernels, pack(): pl.pallas_call(pack_kernel, out_shape=(jax.ShapeDtypeStruct((CLUSTERS, 3...  7.46 us
    all_to_all x1, starting transfers between devices, local(): back = lax.all_to_all(mixed, SEQ, split_axis=0, concat_axis=0, tiled=True)  7.44 us
    ppermute x2, starting transfers between devices, passed_along(): lax.ppermute(value, SEQ, [(s, s + steps) for s in range(count - steps)])  7.43 us
    pallas_call x1, Pallas kernels, windowed(): pl.pallas_call(local_kernel, out_shape=jax.ShapeDtypeStruct((TOK, D), jnp...  5.96 us
  transfers between devices with their start and end apart: 4, of which 3 were waited for; matrix products, arithmetic and copies ran while one was open for 2% of the time, Pallas kernels for 6%

profile of v1, /device:TPU:1, one launch (start us, length us, event | category | flops | bytes accessed | tf_op | source)
XLA Modules:
  0.0 123.5 jit_solution(257715263171896195)
XLA Ops:
  0.6 7.5 %pack_slots.1 = (bf16[32,384,128]{2,1,0:T(8,128)(2,1)}, f32[8,1024]{1,0:T(8,128)}) custom-call(s32[1,1024]{1,0:T(1,128)} %bitcast.18, bf16[1024,128]{1,0:T(8,128)(2,1)} %bitcast.12, bf16[1024,128]{1,0:T(8,128)(2,1)} %bitcast.13, bf16[1024,128]{1,0:T(8,128)(2,1)} %bitcast.14), custom_call_target="tpu_custom_call" | custom-call | tf_op jit(solution)/shard_map/pack_slots/pallas_call | solution.py:68
  8.1 0.0 copy-start.2
  8.1 8.7 %all-to-all-start = ((bf16[32,384,128]{2,1,0:T(8,128)(2,1)}), bf16[32,384,128]{2,1,0:T(8,128)(2,1)S(1)}, u32[]{:S(2)}, u32[]{:S(2)}) async-start(bf16[32,384,128]{2,1,0:T(8,128)(2,1)} %get-tuple-element.11), calls=%async_computation | async-start | bytes 6291456 | tf_op jit(solution)/shard_map/all_to_all | solution.py:264
  16.8 0.0 copy-done.2
  16.8 0.7 constant_dynamic-update-slice_fusion.1
  17.5 1.7 %constant_dynamic-update-slice_fusion = bf16[2,1024,128]{2,1,0:T(8,128)(2,1)} fusion(bf16[2,1024,128]{2,1,0:T(8,128)(2,1)} %constant_dynamic-update-slice_fusion.1, bf16[1,1024,128]{2,1,0:T(8,128)(2,1)} %param.13), kind=kLoop, calls=%fused_computation | loop fusion | bytes 524288 | tf_op jit(solution)/shard_map/concatenate | solution.py:259
  19.2 3.5 %collective-permute-start.1 = (bf16[2,1024,128]{2,1,0:T(8,128)(2,1)}, bf16[2,1024,128]{2,1,0:T(8,128)(2,1)}, u32[]{:S(2)}, u32[]{:S(2)}) collective-permute-start(bf16[2,1024,128]{2,1,0:T(8,128)(2,1)} %constant_dynamic-update-slice_fusion), channel_id=1, source_target_pairs={{0,1},{1,2},{2,3},{3,4},{4,5},{5,6},{6,7},{7,8},{8,9},{9,10},{10,1... | collective-permute-start | bytes 1572872 | tf_op jit(solution)/shard_map/ppermute | solution.py:254
  22.8 3.9 %collective-permute-start = (bf16[2,1024,128]{2,1,0:T(8,128)(2,1)}, bf16[2,1024,128]{2,1,0:T(8,128)(2,1)}, u32[]{:S(2)}, u32[]{:S(2)}) collective-permute-start(bf16[2,1024,128]{2,1,0:T(8,128)(2,1)} %constant_dynamic-update-slice_fusion), channel_id=1, source_target_pairs={{0,2},{1,3},{2,4},{3,5},{4,6},{5,7},{6,8},{7,9},{8,10},{9,11},{10,... | collective-permute-start | bytes 1572872 | tf_op jit(solution)/shard_map/ppermute | solution.py:254
  26.7 36.2 %collective-permute-done.1.near_ref = bf16[2,1024,128]{2,1,0:T(8,128)(2,1)} collective-permute-done((bf16[2,1024,128]{2,1,0:T(8,128)(2,1)}, bf16[2,1024,128]{2,1,0:T(8,128)(2,1)}, u32[]{:S(2)}, u32[]{:S(2)}) %collective-permute-start.1) | collective-permute-done | bytes 524320 | tf_op jit(solution)/shard_map/ppermute | solution.py:254
  62.9 5.9 %collective-permute-done.far_ref = bf16[2,1024,128]{2,1,0:T(8,128)(2,1)} collective-permute-done((bf16[2,1024,128]{2,1,0:T(8,128)(2,1)}, bf16[2,1024,128]{2,1,0:T(8,128)(2,1)}, u32[]{:S(2)}, u32[]{:S(2)}) %collective-permute-start) | collective-permute-done | bytes 524320 | tf_op jit(solution)/shard_map/ppermute | solution.py:254
  68.8 6.0 %window_attention.1 = bf16[1024,128]{1,0:T(8,128)(2,1)} custom-call(s32[1]{0:T(128)} %bitcast.4.at_ref, bf16[1024,128]{1,0:T(8,128)(2,1)} %bitcast.20, bf16[1024,128]{1,0:T(8,128)(2,1)} %bitcast.16, bf16[1024,128]{1,0:T(8,128)(2,1)} %bitcast.17, bf16[2,1024,128]{2,1,0:T(8,128)(2,1)} %collective-permute-done.far_ref, ...), custom_call_target="tpu_custom_call" | custom-call | flops 1207959552 | bytes 2097152 | tf_op jit(solution)/shard_map/window_attention/pallas_call | solution.py:187
  74.7 0.0 all-to-all-done.got_ref
  74.7 0.0 copy-start.1
  74.7 1.6 %copy-done.1 = bf16[32,384,128]{2,1,0:T(8,128)(2,1)} copy-done((bf16[32,384,128]{2,1,0:T(8,128)(2,1)}, bf16[32,384,128]{2,1,0:T(8,128)(2,1)S(1)}, u32[]{:S(2)}) %copy-start.1) | copy-done | bytes 3145752
  76.4 17.4 %cluster_attention.1 = bf16[32,128,128]{2,1,0:T(8,128)(2,1)} custom-call(bf16[32,384,128]{2,1,0:T(8,128)(2,1)} %copy-done.1), custom_call_target="tpu_custom_call" | custom-call | flops 8589934592 | bytes 4194304 | tf_op jit(solution)/shard_map/cluster_attention/pallas_call | solution.py:137
  93.7 7.4 %all-to-all-start.1 = ((bf16[32,128,128]{2,1,0:T(8,128)(2,1)}), bf16[32,128,128]{2,1,0:T(8,128)(2,1)S(1)}, u32[]{:S(2)}, u32[]{:S(2)}) async-start(bf16[32,128,128]{2,1,0:T(8,128)(2,1)} %cluster_attention.1), calls=%async_computation.1 | async-start | bytes 2097152 | tf_op jit(solution)/shard_map/all_to_all | solution.py:271
  101.2 1.8 %slot_columns.1 = (bf16[1024,128]{1,0:T(8,128)(2,1)}, bf16[1024,128]{1,0:T(8,128)(2,1)}) custom-call(s32[1,1024]{1,0:T(1,128)} %bitcast.19, f32[8,1024]{1,0:T(8,128)} %get-tuple-element.8.rank_ref), custom_call_target="tpu_custom_call" | custom-call | tf_op jit(solution)/shard_map/slot_columns/pallas_call | solution.py:213
  103.0 15.1 %all-to-all-done.1 = bf16[32,128,128]{2,1,0:T(8,128)(2,1)S(1)} async-done(((bf16[32,128,128]{2,1,0:T(8,128)(2,1)}), bf16[32,128,128]{2,1,0:T(8,128)(2,1)S(1)}, u32[]{:S(2)}, u32[]{:S(2)}) %all-to-all-start.1) | async-done | bytes 1048608 | tf_op jit(solution)/shard_map/all_to_all | solution.py:271
  118.1 0.0 copy-start
  118.1 1.0 copy-done
  119.1 4.4 %unpack_slots.1 = bf16[1024,128]{1,0:T(8,128)(2,1)} custom-call(bf16[1024,128]{1,0:T(8,128)(2,1)} %get-tuple-element.9.at_rank_ref, bf16[1024,128]{1,0:T(8,128)(2,1)} %get-tuple-element.10.ids_ref, bf16[4096,128]{1,0:T(8,128)(2,1)} %bitcast.11), custom_call_target="tpu_custom_call" | custom-call | tf_op jit(solution)/shard_map/unpack_slots/pallas_call | solution.py:242
Async XLA Ops:
  8.1 8.7 %copy-start.2 = (bf16[1,1024,128]{2,1,0:T(8,128)(2,1)S(1)}, bf16[1,1024,128]{2,1,0:T(8,128)(2,1)}, u32[]{:S(2)}) copy-start(bf16[1,1024,128]{2,1,0:T(8,128)(2,1)} %param.12) | copy-start | bytes 786436
  8.1 66.6 %all-to-all-start = ((bf16[32,384,128]{2,1,0:T(8,128)(2,1)}), bf16[32,384,128]{2,1,0:T(8,128)(2,1)S(1)}, u32[]{:S(2)}, u32[]{:S(2)}) async-start(bf16[32,384,128]{2,1,0:T(8,128)(2,1)} %get-tuple-element.11), calls=%async_computation | async-start | bytes 6291456 | tf_op jit(solution)/shard_map/all_to_all | solution.py:264
  19.2 43.6 %collective-permute-start.1 = (bf16[2,1024,128]{2,1,0:T(8,128)(2,1)}, bf16[2,1024,128]{2,1,0:T(8,128)(2,1)}, u32[]{:S(2)}, u32[]{:S(2)}) collective-permute-start(bf16[2,1024,128]{2,1,0:T(8,128)(2,1)} %constant_dynamic-update-slice_fusion), channel_id=1, source_target_pairs={{0,1},{1,2},{2,3},{3,4},{4,5},{5,6},{6,7},{7,8},{8,9},{9,10},{10,1... | collective-permute-start | bytes 1572872 | tf_op jit(solution)/shard_map/ppermute | solution.py:254
  22.8 46.0 %collective-permute-start = (bf16[2,1024,128]{2,1,0:T(8,128)(2,1)}, bf16[2,1024,128]{2,1,0:T(8,128)(2,1)}, u32[]{:S(2)}, u32[]{:S(2)}) collective-permute-start(bf16[2,1024,128]{2,1,0:T(8,128)(2,1)} %constant_dynamic-update-slice_fusion), channel_id=1, source_target_pairs={{0,2},{1,3},{2,4},{3,5},{4,6},{5,7},{6,8},{7,9},{8,10},{9,11},{10,... | collective-permute-start | bytes 1572872 | tf_op jit(solution)/shard_map/ppermute | solution.py:254
  74.7 1.6 %copy-start.1 = (bf16[32,384,128]{2,1,0:T(8,128)(2,1)}, bf16[32,384,128]{2,1,0:T(8,128)(2,1)S(1)}, u32[]{:S(2)}) copy-start(bf16[32,384,128]{2,1,0:T(8,128)(2,1)S(1)} %all-to-all-done.got_ref) | copy-start | bytes 9437188
  93.7 24.4 %all-to-all-start.1 = ((bf16[32,128,128]{2,1,0:T(8,128)(2,1)}), bf16[32,128,128]{2,1,0:T(8,128)(2,1)S(1)}, u32[]{:S(2)}, u32[]{:S(2)}) async-start(bf16[32,128,128]{2,1,0:T(8,128)(2,1)} %cluster_attention.1), calls=%async_computation.1 | async-start | bytes 2097152 | tf_op jit(solution)/shard_map/all_to_all | solution.py:271
  118.1 1.0 copy-start

commit v2 on v1

--- a/solution.py
+++ b/solution.py
@@ -16,6 +16,7 @@
 NEVER = -1e30
 EMPTY = 256.0
 GROUP = 8
+CHUNK = 1024
 VMEM = pl.BlockSpec(memory_space=pltpu.VMEM)
 
 
@@ -78,24 +79,42 @@
     )(ids, q, k, v)
 
 
-def attend(queries, keys, values, allowed_of):
-    scores = []
-    for piece, allowed in zip(keys, allowed_of):
+def attend(tasks, query_of, key_ref, value_ref, write):
+    def score(task):
+        block, low, high, mask, _, _ = task
         s = lax.dot_general(
-            queries, piece, (((1,), (1,)), ((), ())), preferred_element_type=jnp.float32
-        )
-        scores.append(s if allowed is None else jnp.where(allowed, s, NEVER))
-    top = jnp.max(scores[0], axis=1, keepdims=True)
-    for s in scores[1:]:
-        top = jnp.maximum(top, jnp.max(s, axis=1, keepdims=True))
-    shift = top * EXP_SCALE
-    total = None
-    for s, piece in zip(scores, values):
-        weight = jnp.exp2(s * EXP_SCALE - shift).astype(jnp.bfloat16)
-        part = jnp.dot(weight, piece, preferred_element_type=jnp.float32)
-        total = part if total is None else total + part
-    mass = total[:, D : 2 * D]
-    return (total[:, 0:D] / jnp.where(mass > 0.0, mass, 1.0)).astype(jnp.bfloat16)
+            query_of(block),
+            key_ref[low:high],
+            (((1,), (1,)), ((), ())),
+            preferred_element_type=jnp.float32,
+        )
+        return s if mask is None else jnp.where(mask, s, NEVER)
+
+    coming = score(tasks[0])
+    for t, (block, low, high, _, first, last) in enumerate(tasks):
+        s = coming
+        if t + 1 < len(tasks):
+            coming = score(tasks[t + 1])
+        top = jnp.max(s, axis=1, keepdims=True)
+        if not first:
+            top = jnp.maximum(top, top_before)
+        weight = jnp.exp2(s * EXP_SCALE - top * EXP_SCALE).astype(jnp.bfloat16)
+        total = jnp.dot(weight, value_ref[low:high], preferred_element_type=jnp.float32)
+        if not first:
+            total = total + total_before * jnp.exp2((top_before - top) * EXP_SCALE)
+        top_before, total_before = top, total
+        if last:
+            mass = total[:, D : 2 * D]
+            write(
+                block, (total[:, 0:D] / jnp.where(mass > 0.0, mass, 1.0)).astype(jnp.bfloat16)
+            )
+
+
+def tasks_of(block, spans):
+    return [
+        (block, low, high, mask, t == 0, t == len(spans) - 1)
+        for t, (low, high, mask) in enumerate(spans)
+    ]
 
 
 def routed_kernel(got_ref, out_ref, key_ref, value_ref):
@@ -117,18 +136,22 @@
     within = lax.broadcasted_iota(jnp.int32, (size, size), 1) <= lax.broadcasted_iota(
         jnp.int32, (size, size), 0
     )
+    tasks = []
     for i in range(blocks // 2):
-        low = i * size
-        queries = got_ref[2 * i : 2 * i + 2, 0:CAP].reshape(size, D)
-        keys, values, masks = [], [], []
-        if low > 0:
-            keys.append(key_ref[0:low])
-            values.append(value_ref[0:low])
-            masks.append(None)
-        keys.append(key_ref[low : low + size])
-        values.append(value_ref[low : low + size])
-        masks.append(within)
-        out_ref[2 * i : 2 * i + 2] = attend(queries, keys, values, masks).reshape(2, CAP, D)
+        own = i * size
+        spans = [(low, min(low + CHUNK, own), None) for low in range(0, own, CHUNK)]
+        tasks += tasks_of(i, spans + [(own, own + size, within)])
+
+    def write(i, mixed):
+        out_ref[2 * i : 2 * i + 2] = mixed.reshape(2, CAP, D)
+
+    attend(
+        tasks,
+        lambda i: got_ref[2 * i : 2 * i + 2, 0:CAP].reshape(size, D),
+        key_ref,
+        value_ref,
+        write,
+    )
 
 
 def routed(got):
@@ -151,17 +174,20 @@
     )(got)
 
 
-def local_kernel(at_ref, q_ref, k_ref, v_ref, far_ref, near_ref, out_ref, key_ref, value_ref):
+def local_kernel(
+    at_ref, q_ref, k_ref, v_ref, far_k_ref, far_v_ref, near_ref, out_ref, key_ref, value_ref
+):
     at = at_ref[0]
     own = k_ref[0:16].astype(jnp.float32)[0:1]
     nearest = near_ref[0, 0:16].astype(jnp.float32)[0:1]
-    for b, ref in enumerate((far_ref, near_ref)):
+    earlier = ((far_k_ref[...], far_v_ref[...]), (near_ref[0], near_ref[1]))
+    for b, (key, value) in enumerate(earlier):
         there = at >= 2 - b
         start = jnp.where(at == 0, own, nearest)
         filler = jnp.broadcast_to(start, (TOK, D))
         rows = pl.ds(b * TOK, TOK)
-        key_ref[rows] = jnp.where(there, ref[0].astype(jnp.float32), filler).astype(jnp.bfloat16)
-        value_ref[rows, 0:D] = ref[1]
+        key_ref[rows] = jnp.where(there, key.astype(jnp.float32), filler).astype(jnp.bfloat16)
+        value_ref[rows, 0:D] = value
         value_ref[rows, D : 2 * D] = jnp.full((TOK, D), jnp.where(there, 1.0, 0.0)).astype(
             jnp.bfloat16
         )
@@ -171,23 +197,32 @@
     size = 256
     column = lax.broadcasted_iota(jnp.int32, (size, size), 1)
     line = lax.broadcasted_iota(jnp.int32, (size, size), 0)
+    tasks = []
     for i in range(TOK // size):
         low = i * size
         high = low + 2 * TOK
-        spans = ((low, low + size), (low + size, high), (high, high + size))
-        out_ref[low : low + size] = attend(
-            q_ref[low : low + size],
-            [key_ref[a:b] for a, b in spans],
-            [value_ref[a:b] for a, b in spans],
-            (column > line, None, column <= line),
-        )
-
-
-def windowed(at, q, k, v, far, near):
+        middle = low + size + CHUNK
+        spans = [
+            (low, low + size, column > line),
+            (low + size, middle, None),
+            (middle, high, None),
+            (high, high + size, column <= line),
+        ]
+        tasks += tasks_of(i, spans)
+
+    def write(i, mixed):
+        out_ref[i * size : (i + 1) * size] = mixed
+
+    attend(
+        tasks, lambda i: q_ref[i * size : (i + 1) * size], key_ref, value_ref, write
+    )
+
+
+def windowed(at, q, k, v, far_k, far_v, near):
     return pl.pallas_call(
         local_kernel,
         out_shape=jax.ShapeDtypeStruct((TOK, D), jnp.bfloat16),
-        in_specs=[pl.BlockSpec(memory_space=pltpu.SMEM)] + [VMEM] * 5,
+        in_specs=[pl.BlockSpec(memory_space=pltpu.SMEM)] + [VMEM] * 6,
         out_specs=VMEM,
         scratch_shapes=[
             pltpu.VMEM((3 * TOK, D), jnp.bfloat16),
@@ -198,7 +233,7 @@
             flops=TOK * 2304 * D * 4, bytes_accessed=8 * TOK * D * 2, transcendentals=0
         ),
         name="window_attention",
-    )(at, q, k, v, far, near)
+    )(at, q, k, v, far_k, far_v, near)
 
 
 def slot_kernel(ids_ref, rank_ref, at_rank_ref, ids_col_ref):
@@ -256,15 +291,21 @@
 
 def local(q_routed, k_routed, v_routed, memberships, q_local, k_local, v_local):
     seq_index = lax.axis_index(SEQ)
-    pair = jnp.concatenate([k_local, v_local], axis=0)
-    far = passed_along(pair, 2)
-    near = passed_along(pair, 1)
+    far_k = passed_along(k_local, 2)
+    far_v = passed_along(v_local, 2)
     ids = memberships.reshape(1, TOK)
     sent, rank = pack(ids, q_routed[0], k_routed[0], v_routed[0])
+    sent, far_k, far_v = lax.optimization_barrier((sent, far_k, far_v))
+    given = jnp.where(
+        seq_index % 2 == 1,
+        jnp.concatenate([far_k, far_v], axis=0),
+        jnp.concatenate([k_local, v_local], axis=0),
+    )
+    near = lax.ppermute(given, SEQ, [(s, s ^ 1) for s in range(lax.axis_size(SEQ))])
     got = lax.all_to_all(sent, SEQ, split_axis=0, concat_axis=0, tiled=True)
     at_rank, ids_col = slots(ids, rank)
     out_local = windowed(
-        seq_index.astype(jnp.int32).reshape(1), q_local[0], k_local[0], v_local[0], far, near
+        seq_index.astype(jnp.int32).reshape(1), q_local[0], k_local[0], v_local[0], far_k[0], far_v[0], near
     )
     got, out_local = lax.optimization_barrier((got, out_local))
     mixed = routed(got)

time: 124 us -> 110 us (0.89)
  waiting for transfers between devices: 57.2 us -> 46.8 us
  Pallas kernels: 37 us -> 34.5 us
  starting transfers between devices: 23.6 us -> 22.2 us
    ppermute x2, waiting for transfers between devices: 42.1 us -> 0.19 us  [passed_along(): lax.ppermute(value, SEQ, [(s, s + steps) for s in range(count - steps)])]
    all_to_all x1, waiting for transfers between devices: 0.01 us -> 29.9 us  [local(): got = lax.all_to_all(sent, SEQ, split_axis=0, concat_axis=0, tiled=True)]
    all_to_all x1, starting transfers between devices: 7.44 us -> 4.98 us  [local(): back = lax.all_to_all(mixed, SEQ, split_axis=0, concat_axis=0, tiled=True)]
    pallas_call x1, Pallas kernels: 17.4 us -> 15.2 us  [routed(): pl.pallas_call(routed_kernel, out_shape=jax.ShapeDtypeStruct((blocks, CAP...]
    concatenate x1 -> x0, local copies, waits for them, and re-layouts: 1.68 us -> none  [local(): pair = jnp.concatenate([k_local, v_local], axis=0)]
    ppermute x0 -> x1, waiting for transfers between devices: none -> 1.67 us  [local(): lax.ppermute(given, SEQ, [(s, s ^ 1) for s in range(lax.axis_size(SEQ))])]
    unnamed x7 -> x12, local copies, waits for them, and re-layouts: 3.33 us -> 4.15 us
  transfers between devices with their start and end apart: 4 -> 5, of which waited for: 3 -> 4; matrix products, arithmetic and copies ran while one was open for 2% -> 1% of each run, Pallas kernels for 6% -> 14%
where the time goes in v2:
time: 110 us
  waiting for transfers between devices  46.8 us (43%)
  Pallas kernels  34.5 us (31%)
  starting transfers between devices  22.2 us (20%)
  local copies, waits for them, and re-layouts  4.15 us (4%)
  other arithmetic  1.2 us (1%)
    all_to_all x1, waiting for transfers between devices, local(): got = lax.all_to_all(sent, SEQ, split_axis=0, concat_axis=0, tiled=True)  29.9 us
    pallas_call x1, Pallas kernels, routed(): pl.pallas_call(routed_kernel, out_shape=jax.ShapeDtypeStruct((blocks, CAP...  15.2 us
    all_to_all x1, waiting for transfers between devices, local(): back = lax.all_to_all(mixed, SEQ, split_axis=0, concat_axis=0, tiled=True)  15.1 us
    all_to_all x1, starting transfers between devices, local(): got = lax.all_to_all(sent, SEQ, split_axis=0, concat_axis=0, tiled=True)  9.43 us
    pallas_call x1, Pallas kernels, pack(): pl.pallas_call(pack_kernel, out_shape=(jax.ShapeDtypeStruct((CLUSTERS, 3...  7.47 us
    ppermute x2, starting transfers between devices, passed_along(): lax.ppermute(value, SEQ, [(s, s + steps) for s in range(count - steps)])  7.25 us
    pallas_call x1, Pallas kernels, windowed(): pl.pallas_call(local_kernel, out_shape=jax.ShapeDtypeStruct((TOK, D), jnp...  5.67 us
    all_to_all x1, starting transfers between devices, local(): back = lax.all_to_all(mixed, SEQ, split_axis=0, concat_axis=0, tiled=True)  4.98 us
  transfers between devices with their start and end apart: 5, of which 4 were waited for; matrix products, arithmetic and copies ran while one was open for 1% of the time, Pallas kernels for 14%

profile of v2, /device:TPU:1, one launch (start us, length us, event | category | flops | bytes accessed | tf_op | source)
XLA Modules:
  0.0 109.6 jit_solution(10564993619235664726)
XLA Ops:
  0.6 4.0 %collective-permute-start = (bf16[1,1024,128]{2,1,0:T(8,128)(2,1)}, bf16[1,1024,128]{2,1,0:T(8,128)(2,1)S(1)}, u32[]{:S(2)}, u32[]{:S(2)}) collective-permute-start(bf16[1,1024,128]{2,1,0:T(8,128)(2,1)} %param.12), channel_id=1, source_target_pairs={{0,2},{1,3},{2,4},{3,5},{4,6},{5,7},{6,8},{7,9},{8,10},{9,11},{10,... | collective-permute-start | bytes 786440 | tf_op jit(solution)/shard_map/ppermute | solution.py:289
  4.7 3.2 %collective-permute-start.1 = (bf16[1,1024,128]{2,1,0:T(8,128)(2,1)}, bf16[1,1024,128]{2,1,0:T(8,128)(2,1)S(1)}, u32[]{:S(2)}, u32[]{:S(2)}) collective-permute-start(bf16[1,1024,128]{2,1,0:T(8,128)(2,1)} %param.13), channel_id=1, source_target_pairs={{0,2},{1,3},{2,4},{3,5},{4,6},{5,7},{6,8},{7,9},{8,10},{9,11},{10,... | collective-permute-start | bytes 786440 | tf_op jit(solution)/shard_map/ppermute | solution.py:289
  7.9 7.5 %pack_slots.1 = (bf16[32,384,128]{2,1,0:T(8,128)(2,1)}, f32[8,1024]{1,0:T(8,128)}) custom-call(s32[1,1024]{1,0:T(1,128)} %bitcast.22, bf16[1024,128]{1,0:T(8,128)(2,1)} %bitcast.14, bf16[1024,128]{1,0:T(8,128)(2,1)} %bitcast.15, bf16[1024,128]{1,0:T(8,128)(2,1)} %bitcast.16), custom_call_target="tpu_custom_call" | custom-call | tf_op jit(solution)/shard_map/pack_slots/pallas_call | solution.py:69
  15.4 0.0 collective-permute-done
  15.4 0.0 copy-start.3
  15.4 0.2 collective-permute-done.1
  15.6 0.0 copy-start.4
  15.6 0.5 copy-done.3
  16.1 0.2 copy-done.4
  16.3 9.4 %all-to-all-start = ((bf16[32,384,128]{2,1,0:T(8,128)(2,1)}), bf16[32,384,128]{2,1,0:T(8,128)(2,1)S(1)}, u32[]{:S(2)}, u32[]{:S(2)}) async-start(bf16[32,384,128]{2,1,0:T(8,128)(2,1)} %get-tuple-element.15), calls=%async_computation | async-start | bytes 6291456 | tf_op jit(solution)/shard_map/all_to_all | solution.py:305
  25.7 0.0 copy-done.2
  25.8 1.2 %maximum_select_fusion = bf16[2,1024,128]{2,1,0:T(8,128)(2,1)S(1)} fusion(bf16[1,1024,128]{2,1,0:T(8,128)(2,1)} %copy-done.4, bf16[1,1024,128]{2,1,0:T(8,128)(2,1)} %copy-done.3, bf16[1,1024,128]{2,1,0:T(8,128)(2,1)} %param.13, bf16[1,1024,128]{2,1,0:T(8,128)(2,1)S(1)} %copy-done.2, pred[]{:T(512)S(6)} %eq.5), kind=kLoop, calls=%fused_computation | loop fusion | flops 786432 | bytes 1572865 | tf_op jit(solution)/shard_map/jit(_where)/select_n | solution.py:299
  27.0 0.5 collective-permute-start.2
  27.5 1.7 %collective-permute-done.2.near_ref = bf16[2,1024,128]{2,1,0:T(8,128)(2,1)S(1)} collective-permute-done((bf16[2,1024,128]{2,1,0:T(8,128)(2,1)S(1)}, bf16[2,1024,128]{2,1,0:T(8,128)(2,1)S(1)}, u32[]{:S(2)}, u32[]{:S(2)}) %collective-permute-start.2) | collective-permute-done | bytes 524320 | tf_op jit(solution)/shard_map/ppermute | solution.py:304
  29.1 0.8 copy-done.5
  29.9 5.7 %window_attention.1 = bf16[1024,128]{1,0:T(8,128)(2,1)} custom-call(s32[1]{0:T(128)} %bitcast.4.at_ref, bf16[1024,128]{1,0:T(8,128)(2,1)} %bitcast.24, bf16[1024,128]{1,0:T(8,128)(2,1)} %bitcast.18, bf16[1024,128]{1,0:T(8,128)(2,1)} %bitcast.19, bf16[1024,128]{1,0:T(8,128)(2,1)} %bitcast.20, bf16[1024,128]{1,0:T(8,128)(2,1)} %bitcast.21, ...), custom_call_target="tpu_custom_call" | custom-call | flops 1207959552 | bytes 2097152 | tf_op jit(solution)/shard_map/window_attention/pallas_call | solution.py:222
  35.6 29.9 %all-to-all-done.got_ref = bf16[32,384,128]{2,1,0:T(8,128)(2,1)S(1)} async-done(((bf16[32,384,128]{2,1,0:T(8,128)(2,1)}), bf16[32,384,128]{2,1,0:T(8,128)(2,1)S(1)}, u32[]{:S(2)}, u32[]{:S(2)}) %all-to-all-start) | async-done | bytes 3145760 | tf_op jit(solution)/shard_map/all_to_all | solution.py:305
  65.5 1.6 %copy-done.1 = bf16[32,384,128]{2,1,0:T(8,128)(2,1)} copy-done((bf16[32,384,128]{2,1,0:T(8,128)(2,1)}, bf16[32,384,128]{2,1,0:T(8,128)(2,1)S(1)}, u32[]{:S(2)}) %copy-start.1) | copy-done | bytes 3145752
  67.1 15.2 %cluster_attention.1 = bf16[32,128,128]{2,1,0:T(8,128)(2,1)} custom-call(bf16[32,384,128]{2,1,0:T(8,128)(2,1)} %copy-done.1), custom_call_target="tpu_custom_call" | custom-call | flops 8589934592 | bytes 4194304 | tf_op jit(solution)/shard_map/cluster_attention/pallas_call | solution.py:160
  82.3 5.0 %all-to-all-start.1 = ((bf16[32,128,128]{2,1,0:T(8,128)(2,1)}), bf16[32,128,128]{2,1,0:T(8,128)(2,1)S(1)}, u32[]{:S(2)}, u32[]{:S(2)}) async-start(bf16[32,128,128]{2,1,0:T(8,128)(2,1)} %cluster_attention.1), calls=%async_computation.1 | async-start | bytes 2097152 | tf_op jit(solution)/shard_map/all_to_all | solution.py:312
  87.3 1.8 %slot_columns.1 = (bf16[1024,128]{1,0:T(8,128)(2,1)}, bf16[1024,128]{1,0:T(8,128)(2,1)}) custom-call(s32[1,1024]{1,0:T(1,128)} %bitcast.23, f32[8,1024]{1,0:T(8,128)} %get-tuple-element.11.rank_ref), custom_call_target="tpu_custom_call" | custom-call | tf_op jit(solution)/shard_map/slot_columns/pallas_call | solution.py:248
  89.1 15.1 %all-to-all-done.1 = bf16[32,128,128]{2,1,0:T(8,128)(2,1)S(1)} async-done(((bf16[32,128,128]{2,1,0:T(8,128)(2,1)}), bf16[32,128,128]{2,1,0:T(8,128)(2,1)S(1)}, u32[]{:S(2)}, u32[]{:S(2)}) %all-to-all-start.1) | async-done | bytes 1048608 | tf_op jit(solution)/shard_map/all_to_all | solution.py:312
  104.2 1.0 copy-done
  105.2 4.4 %unpack_slots.1 = bf16[1024,128]{1,0:T(8,128)(2,1)} custom-call(bf16[1024,128]{1,0:T(8,128)(2,1)} %get-tuple-element.12.at_rank_ref, bf16[1024,128]{1,0:T(8,128)(2,1)} %get-tuple-element.13.ids_ref, bf16[4096,128]{1,0:T(8,128)(2,1)} %bitcast.13), custom_call_target="tpu_custom_call" | custom-call | tf_op jit(solution)/shard_map/unpack_slots/pallas_call | solution.py:277
  (4 shorter events, 0.0 us)
Async XLA Ops:
  0.6 14.7 %collective-permute-start = (bf16[1,1024,128]{2,1,0:T(8,128)(2,1)}, bf16[1,1024,128]{2,1,0:T(8,128)(2,1)S(1)}, u32[]{:S(2)}, u32[]{:S(2)}) collective-permute-start(bf16[1,1024,128]{2,1,0:T(8,128)(2,1)} %param.12), channel_id=1, source_target_pairs={{0,2},{1,3},{2,4},{3,5},{4,6},{5,7},{6,8},{7,9},{8,10},{9,11},{10,... | collective-permute-start | bytes 786440 | tf_op jit(solution)/shard_map/ppermute | solution.py:289
  4.7 10.9 %collective-permute-start.1 = (bf16[1,1024,128]{2,1,0:T(8,128)(2,1)}, bf16[1,1024,128]{2,1,0:T(8,128)(2,1)S(1)}, u32[]{:S(2)}, u32[]{:S(2)}) collective-permute-start(bf16[1,1024,128]{2,1,0:T(8,128)(2,1)} %param.13), channel_id=1, source_target_pairs={{0,2},{1,3},{2,4},{3,5},{4,6},{5,7},{6,8},{7,9},{8,10},{9,11},{10,... | collective-permute-start | bytes 786440 | tf_op jit(solution)/shard_map/ppermute | solution.py:289
  15.4 0.7 copy-start.3
  15.6 0.7 copy-start.4
  15.6 10.2 %copy-start.2 = (bf16[1,1024,128]{2,1,0:T(8,128)(2,1)S(1)}, bf16[1,1024,128]{2,1,0:T(8,128)(2,1)}, u32[]{:S(2)}) copy-start(bf16[1,1024,128]{2,1,0:T(8,128)(2,1)} %param.12) | copy-start | bytes 786436
  16.3 49.2 %all-to-all-start = ((bf16[32,384,128]{2,1,0:T(8,128)(2,1)}), bf16[32,384,128]{2,1,0:T(8,128)(2,1)S(1)}, u32[]{:S(2)}, u32[]{:S(2)}) async-start(bf16[32,384,128]{2,1,0:T(8,128)(2,1)} %get-tuple-element.15), calls=%async_computation | async-start | bytes 6291456 | tf_op jit(solution)/shard_map/all_to_all | solution.py:305
  27.0 2.2 %collective-permute-start.2 = (bf16[2,1024,128]{2,1,0:T(8,128)(2,1)S(1)}, bf16[2,1024,128]{2,1,0:T(8,128)(2,1)S(1)}, u32[]{:S(2)}, u32[]{:S(2)}) collective-permute-start(bf16[2,1024,128]{2,1,0:T(8,128)(2,1)S(1)} %maximum_select_fusion), channel_id=1, source_target_pairs={{0,1},{1,0},{2,3},{3,2},{4,5},{5,4},{6,7},{7,6},{8,9},{9,8},{10,11... | collective-permute-start | bytes 1572872 | tf_op jit(solution)/shard_map/ppermute | solution.py:304
  29.1 0.8 copy-start.5
  65.5 1.6 %copy-start.1 = (bf16[32,384,128]{2,1,0:T(8,128)(2,1)}, bf16[32,384,128]{2,1,0:T(8,128)(2,1)S(1)}, u32[]{:S(2)}) copy-start(bf16[32,384,128]{2,1,0:T(8,128)(2,1)S(1)} %all-to-all-done.got_ref) | copy-start | bytes 9437188
  82.3 21.9 %all-to-all-start.1 = ((bf16[32,128,128]{2,1,0:T(8,128)(2,1)}), bf16[32,128,128]{2,1,0:T(8,128)(2,1)S(1)}, u32[]{:S(2)}, u32[]{:S(2)}) async-start(bf16[32,128,128]{2,1,0:T(8,128)(2,1)} %cluster_attention.1), calls=%async_computation.1 | async-start | bytes 2097152 | tf_op jit(solution)/shard_map/all_to_all | solution.py:312
  104.2 1.0 copy-start

commit v3 on v2

--- a/solution.py
+++ b/solution.py
@@ -20,8 +20,12 @@
 VMEM = pl.BlockSpec(memory_space=pltpu.VMEM)
 
 
+def in_vmem(array):
+    return pltpu.with_memory_space_constraint(array, pltpu.VMEM)
+
+
 def params():
-    return pltpu.CompilerParams(vmem_limit_bytes=56 * 1024 * 1024)
+    return pltpu.CompilerParams(vmem_limit_bytes=40 * 1024 * 1024)
 
 
 def pack_kernel(ids_ref, q_ref, k_ref, v_ref, sent_ref, rank_ref):
@@ -70,7 +74,7 @@
         pack_kernel,
         out_shape=(
             jax.ShapeDtypeStruct((CLUSTERS, 3 * CAP, D), jnp.bfloat16),
-            jax.ShapeDtypeStruct((8, TOK), jnp.float32),
+            pltpu.VMEM((8, TOK), jnp.float32),
         ),
         in_specs=[VMEM] * 4,
         out_specs=(VMEM, VMEM),
@@ -171,16 +175,16 @@
             flops=2 * slots * slots * D * 2, bytes_accessed=4 * slots * D * 2, transcendentals=0
         ),
         name="cluster_attention",
-    )(got)
+    )(in_vmem(got))
 
 
 def local_kernel(
-    at_ref, q_ref, k_ref, v_ref, far_k_ref, far_v_ref, near_ref, out_ref, key_ref, value_ref
+    at_ref, q_ref, k_ref, v_ref, far_ref, near_ref, out_ref, key_ref, value_ref
 ):
     at = at_ref[0]
     own = k_ref[0:16].astype(jnp.float32)[0:1]
     nearest = near_ref[0, 0:16].astype(jnp.float32)[0:1]
-    earlier = ((far_k_ref[...], far_v_ref[...]), (near_ref[0], near_ref[1]))
+    earlier = ((far_ref[0], far_ref[1]), (near_ref[0], near_ref[1]))
     for b, (key, value) in enumerate(earlier):
         there = at >= 2 - b
         start = jnp.where(at == 0, own, nearest)
@@ -218,11 +222,11 @@
     )
 
 
-def windowed(at, q, k, v, far_k, far_v, near):
+def windowed(at, q, k, v, far, near):
     return pl.pallas_call(
         local_kernel,
         out_shape=jax.ShapeDtypeStruct((TOK, D), jnp.bfloat16),
-        in_specs=[pl.BlockSpec(memory_space=pltpu.SMEM)] + [VMEM] * 6,
+        in_specs=[pl.BlockSpec(memory_space=pltpu.SMEM)] + [VMEM] * 5,
         out_specs=VMEM,
         scratch_shapes=[
             pltpu.VMEM((3 * TOK, D), jnp.bfloat16),
@@ -233,7 +237,7 @@
             flops=TOK * 2304 * D * 4, bytes_accessed=8 * TOK * D * 2, transcendentals=0
         ),
         name="window_attention",
-    )(at, q, k, v, far_k, far_v, near)
+    )(at, q, k, v, in_vmem(far), in_vmem(near))
 
 
 def slot_kernel(ids_ref, rank_ref, at_rank_ref, ids_col_ref):
@@ -248,14 +252,14 @@
     return pl.pallas_call(
         slot_kernel,
         out_shape=(
-            jax.ShapeDtypeStruct((TOK, CAP), jnp.bfloat16),
-            jax.ShapeDtypeStruct((TOK, CAP), jnp.bfloat16),
+            pltpu.VMEM((TOK, CAP), jnp.bfloat16),
+            pltpu.VMEM((TOK, CAP), jnp.bfloat16),
         ),
         in_specs=[VMEM] * 2,
         out_specs=(VMEM, VMEM),
         compiler_params=params(),
         name="slot_columns",
-    )(ids, rank)
+    )(ids, in_vmem(rank))
 
 
 def unpack_kernel(at_rank_ref, ids_ref, back_ref, out_ref):
@@ -281,7 +285,7 @@
         out_specs=VMEM,
         compiler_params=params(),
         name="unpack_slots",
-    )(at_rank, ids_col, back)
+    )(in_vmem(at_rank), in_vmem(ids_col), in_vmem(back))
 
 
 def passed_along(value, steps):
@@ -291,25 +295,22 @@
 
 def local(q_routed, k_routed, v_routed, memberships, q_local, k_local, v_local):
     seq_index = lax.axis_index(SEQ)
-    far_k = passed_along(k_local, 2)
-    far_v = passed_along(v_local, 2)
     ids = memberships.reshape(1, TOK)
     sent, rank = pack(ids, q_routed[0], k_routed[0], v_routed[0])
-    sent, far_k, far_v = lax.optimization_barrier((sent, far_k, far_v))
-    given = jnp.where(
-        seq_index % 2 == 1,
-        jnp.concatenate([far_k, far_v], axis=0),
-        jnp.concatenate([k_local, v_local], axis=0),
-    )
+    got = lax.all_to_all(sent, SEQ, split_axis=0, concat_axis=0, tiled=True)
+    pair = jnp.concatenate([k_local, v_local], axis=0)
+    at_rank, ids_col = slots(ids, rank)
+    got, pair, at_rank, ids_col = lax.optimization_barrier((got, pair, at_rank, ids_col))
+    far = passed_along(pair, 2)
+    mixed = routed(got)
+    mixed, far = lax.optimization_barrier((mixed, far))
+    back = lax.all_to_all(mixed, SEQ, split_axis=0, concat_axis=0, tiled=True)
+    given = jnp.where(seq_index % 2 == 1, far, pair)
     near = lax.ppermute(given, SEQ, [(s, s ^ 1) for s in range(lax.axis_size(SEQ))])
-    got = lax.all_to_all(sent, SEQ, split_axis=0, concat_axis=0, tiled=True)
-    at_rank, ids_col = slots(ids, rank)
     out_local = windowed(
-        seq_index.astype(jnp.int32).reshape(1), q_local[0], k_local[0], v_local[0], far_k[0], far_v[0], near
-    )
-    got, out_local = lax.optimization_barrier((got, out_local))
-    mixed = routed(got)
-    back = lax.all_to_all(mixed, SEQ, split_axis=0, concat_axis=0, tiled=True)
+        seq_index.astype(jnp.int32).reshape(1), q_local[0], k_local[0], v_local[0], far, near
+    )
+    back, out_local = lax.optimization_barrier((back, out_local))
     out_routed = unpack(at_rank, ids_col, back.reshape(CLUSTERS * CAP, D))
     return (out_routed[None], out_local[None])
 

time: 110 us -> 102 us (0.927)
  Pallas kernels: 34.5 us -> 25.6 us
  starting transfers between devices: 22.2 us -> 18.3 us
  local copies, waits for them, and re-layouts: 4.15 us -> 6.85 us
  other arithmetic: 1.2 us -> 3.01 us
    all_to_all x1, waiting for transfers between devices: 29.9 us -> 36.9 us  [local(): got = lax.all_to_all(sent, SEQ, split_axis=0, concat_axis=0, tiled=True)]
    all_to_all x1, waiting for transfers between devices: 15.1 us -> 8.44 us  [local(): back = lax.all_to_all(mixed, SEQ, split_axis=0, concat_axis=0, tiled=True)]
    ppermute x2 -> x1, starting transfers between devices: 7.25 us -> 3.33 us  [passed_along(): lax.ppermute(value, SEQ, [(s, s + steps) for s in range(count - steps)])]
    pallas_call x1, Pallas kernels: 15.2 us -> 12.3 us  [routed(): pl.pallas_call(routed_kernel, out_shape=jax.ShapeDtypeStruct((blocks, CAP...]
    pallas_call x1, Pallas kernels: 7.47 us -> 4.69 us  [pack(): pl.pallas_call(pack_kernel, out_shape=(jax.ShapeDtypeStruct((CLUSTERS, 3...]
    unnamed x12 -> x24, local copies, waits for them, and re-layouts: 4.15 us -> 6.85 us
    concatenate x0 -> x1, other arithmetic: none -> 1.87 us  [local(): pair = jnp.concatenate([k_local, v_local], axis=0)]
    pallas_call x1, Pallas kernels: 1.82 us -> 0.27 us  [slots(): pl.pallas_call(slot_kernel, out_shape=(pltpu.VMEM((TOK, CAP), jnp.bfloat1...]
  transfers between devices with their start and end apart: 5 -> 4, of which waited for: 4 -> 3; matrix products, arithmetic and copies ran while one was open for 1% -> 3% of each run, Pallas kernels for 14% -> 18%
where the time goes in v3:
time: 102 us
  waiting for transfers between devices  47 us (46%)
  Pallas kernels  25.6 us (25%)
  starting transfers between devices  18.3 us (18%)
  local copies, waits for them, and re-layouts  6.85 us (7%)
  other arithmetic  3.01 us (3%)
    all_to_all x1, waiting for transfers between devices, local(): got = lax.all_to_all(sent, SEQ, split_axis=0, concat_axis=0, tiled=True)  36.9 us
    pallas_call x1, Pallas kernels, routed(): pl.pallas_call(routed_kernel, out_shape=jax.ShapeDtypeStruct((blocks, CAP...  12.3 us
    all_to_all x1, starting transfers between devices, local(): got = lax.all_to_all(sent, SEQ, split_axis=0, concat_axis=0, tiled=True)  8.72 us
    all_to_all x1, waiting for transfers between devices, local(): back = lax.all_to_all(mixed, SEQ, split_axis=0, concat_axis=0, tiled=True)  8.44 us
    unnamed x24, local copies, waits for them, and re-layouts  6.85 us
    all_to_all x1, starting transfers between devices, local(): back = lax.all_to_all(mixed, SEQ, split_axis=0, concat_axis=0, tiled=True)  5.96 us
    pallas_call x1, Pallas kernels, windowed(): pl.pallas_call(local_kernel, out_shape=jax.ShapeDtypeStruct((TOK, D), jnp...  5.29 us
    pallas_call x1, Pallas kernels, pack(): pl.pallas_call(pack_kernel, out_shape=(jax.ShapeDtypeStruct((CLUSTERS, 3...  4.69 us
  transfers between devices with their start and end apart: 4, of which 3 were waited for; matrix products, arithmetic and copies ran while one was open for 3% of the time, Pallas kernels for 18%

profile of v3, /device:TPU:1, one launch (start us, length us, event | category | flops | bytes accessed | tf_op | source)
XLA Modules:
  0.0 101.5 jit_solution(7739323491484068382)
XLA Ops:
  0.6 0.9 copy-done.2
  1.6 0.9 copy-done.3
  2.5 0.9 copy-done.4
  3.5 0.7 copy-done.9
  4.2 4.7 %pack_slots.1 = (bf16[32,384,128]{2,1,0:T(8,128)(2,1)S(1)}, f32[8,1024]{1,0:T(8,128)S(1)}) custom-call(s32[1,1024]{1,0:T(1,128)S(1)} %bitcast.17, bf16[1024,128]{1,0:T(8,128)(2,1)S(1)} %bitcast.12, bf16[1024,128]{1,0:T(8,128)(2,1)S(1)} %bitcast.13, bf16[1024,128]{1,0:T(8,128)(2,1)S(1)} %bitcast.14), custom_call_target="tpu_custom_call" | custom-call | tf_op jit(solution)/shard_map/pack_slots/pallas_call | solution.py:73
  8.9 1.6 %copy-done = bf16[32,384,128]{2,1,0:T(8,128)(2,1)} copy-done((bf16[32,384,128]{2,1,0:T(8,128)(2,1)}, bf16[32,384,128]{2,1,0:T(8,128)(2,1)S(1)}, u32[]{:S(2)}) %copy-start) | copy-done | bytes 3145752
  10.5 8.7 %all-to-all-start = ((bf16[32,384,128]{2,1,0:T(8,128)(2,1)}), bf16[32,384,128]{2,1,0:T(8,128)(2,1)S(1)}, u32[]{:S(2)}, u32[]{:S(2)}) async-start(bf16[32,384,128]{2,1,0:T(8,128)(2,1)} %copy-done), calls=%async_computation | async-start | bytes 6291456 | tf_op jit(solution)/shard_map/all_to_all | solution.py:300
  19.2 0.3 slot_columns.1
  19.5 0.0 copy-start.5
  19.5 0.7 copy-done.5
  20.2 1.9 %pad_maximum_fusion = bf16[2,1024,128]{2,1,0:T(8,128)(2,1)} fusion(bf16[1,1024,128]{2,1,0:T(8,128)(2,1)} %param.13, bf16[1,1024,128]{2,1,0:T(8,128)(2,1)} %param.12), kind=kLoop, calls=%fused_computation | loop fusion | flops 262144 | bytes 1048576 | tf_op jit(solution)/shard_map/concatenate | solution.py:301
  22.1 36.9 %all-to-all-done.got_ref = bf16[32,384,128]{2,1,0:T(8,128)(2,1)S(1)} async-done(((bf16[32,384,128]{2,1,0:T(8,128)(2,1)}), bf16[32,384,128]{2,1,0:T(8,128)(2,1)S(1)}, u32[]{:S(2)}, u32[]{:S(2)}) %all-to-all-start) | async-done | bytes 3145760 | tf_op jit(solution)/shard_map/all_to_all | solution.py:300
  59.0 3.3 %collective-permute-start = (bf16[2,1024,128]{2,1,0:T(8,128)(2,1)}, bf16[2,1024,128]{2,1,0:T(8,128)(2,1)}, u32[]{:S(2)}, u32[]{:S(2)}) collective-permute-start(bf16[2,1024,128]{2,1,0:T(8,128)(2,1)} %pad_maximum_fusion), channel_id=1, source_target_pairs={{0,2},{1,3},{2,4},{3,5},{4,6},{5,7},{6,8},{7,9},{8,10},{9,11},{10,... | collective-permute-start | bytes 1572872 | tf_op jit(solution)/shard_map/ppermute | solution.py:293
  62.3 12.3 %cluster_attention.1 = bf16[32,128,128]{2,1,0:T(8,128)(2,1)S(1)} custom-call(bf16[32,384,128]{2,1,0:T(8,128)(2,1)S(1)} %all-to-all-done.got_ref), custom_call_target="tpu_custom_call" | custom-call | flops 8589934592 | bytes 4194304 | tf_op jit(solution)/shard_map/cluster_attention/pallas_call | solution.py:164
  74.6 1.0 copy-done.1
  75.6 0.0 collective-permute-done.far_ref
  75.6 6.0 %all-to-all-start.1 = ((bf16[32,128,128]{2,1,0:T(8,128)(2,1)}), bf16[32,128,128]{2,1,0:T(8,128)(2,1)S(1)}, u32[]{:S(2)}, u32[]{:S(2)}) async-start(bf16[32,128,128]{2,1,0:T(8,128)(2,1)} %copy-done.1), calls=%async_computation.1 | async-start | bytes 2097152 | tf_op jit(solution)/shard_map/all_to_all | solution.py:307
  81.6 0.0 copy-start.6
  81.6 1.1 %broadcast_select_fusion = bf16[2,1024,128]{2,1,0:T(8,128)(2,1)S(1)} fusion(bf16[2,1024,128]{2,1,0:T(8,128)(2,1)} %collective-permute-done.far_ref, bf16[2,1024,128]{2,1,0:T(8,128)(2,1)} %pad_maximum_fusion, pred[]{:T(512)S(6)} %eq.5), kind=kLoop, calls=%fused_computation.1 | loop fusion | flops 262144 | bytes 1572865 | tf_op jit(solution)/shard_map/jit(_where)/select_n | solution.py:308
  82.7 0.3 collective-permute-start.1
  83.1 1.7 %collective-permute-done.1.near_ref = bf16[2,1024,128]{2,1,0:T(8,128)(2,1)S(1)} collective-permute-done((bf16[2,1024,128]{2,1,0:T(8,128)(2,1)S(1)}, bf16[2,1024,128]{2,1,0:T(8,128)(2,1)S(1)}, u32[]{:S(2)}, u32[]{:S(2)}) %collective-permute-start.1) | collective-permute-done | bytes 524320 | tf_op jit(solution)/shard_map/ppermute | solution.py:309
  84.8 5.3 %window_attention.1 = bf16[1024,128]{1,0:T(8,128)(2,1)} custom-call(s32[1]{0:T(128)} %bitcast.4.at_ref, bf16[1024,128]{1,0:T(8,128)(2,1)S(1)} %bitcast.19, bf16[1024,128]{1,0:T(8,128)(2,1)S(1)} %bitcast.15, bf16[1024,128]{1,0:T(8,128)(2,1)S(1)} %bitcast.16, bf16[2,1024,128]{2,1,0:T(8,128)(2,1)} %collective-permute-done.far_ref, ...), custom_call_target="tpu_custom_call" | custom-call | flops 1207959552 | bytes 2097152 | tf_op jit(solution)/shard_map/window_attention/pallas_call | solution.py:226
  90.0 8.4 %all-to-all-done.1 = bf16[32,128,128]{2,1,0:T(8,128)(2,1)S(1)} async-done(((bf16[32,128,128]{2,1,0:T(8,128)(2,1)}), bf16[32,128,128]{2,1,0:T(8,128)(2,1)S(1)}, u32[]{:S(2)}, u32[]{:S(2)}) %all-to-all-start.1) | async-done | bytes 1048608 | tf_op jit(solution)/shard_map/all_to_all | solution.py:307
  98.5 3.0 %unpack_slots.1 = bf16[1024,128]{1,0:T(8,128)(2,1)} custom-call(bf16[1024,128]{1,0:T(8,128)(2,1)S(1)} %get-tuple-element.18.at_rank_ref, bf16[1024,128]{1,0:T(8,128)(2,1)S(1)} %copy-done.6, bf16[4096,128]{1,0:T(8,128)(2,1)S(1)} %bitcast.11), custom_call_target="tpu_custom_call" | custom-call | tf_op jit(solution)/shard_map/unpack_slots/pallas_call | solution.py:281
  (15 shorter events, 0.0 us)
Async XLA Ops:
  0.6 1.0 copy-start.2
  1.6 0.9 copy-start.3
  2.5 0.9 copy-start.4
  3.5 0.7 copy-start.9
  8.9 1.6 %copy-start = (bf16[32,384,128]{2,1,0:T(8,128)(2,1)}, bf16[32,384,128]{2,1,0:T(8,128)(2,1)S(1)}, u32[]{:S(2)}) copy-start(bf16[32,384,128]{2,1,0:T(8,128)(2,1)S(1)} %get-tuple-element.14) | copy-start | bytes 9437188
  10.5 8.7 %copy-start.10 = (s32[1,1024,1]{1,2,0:T(1,128)S(1)}, s32[1,1024,1]{1,2,0:T(1,128)}, u32[]{:S(2)}) copy-start(s32[1,1024,1]{1,2,0:T(1,128)} %param.10) | copy-start | bytes 12292
  10.5 48.5 %all-to-all-start = ((bf16[32,384,128]{2,1,0:T(8,128)(2,1)}), bf16[32,384,128]{2,1,0:T(8,128)(2,1)S(1)}, u32[]{:S(2)}, u32[]{:S(2)}) async-start(bf16[32,384,128]{2,1,0:T(8,128)(2,1)} %copy-done), calls=%async_computation | async-start | bytes 6291456 | tf_op jit(solution)/shard_map/all_to_all | solution.py:300
  19.5 0.7 copy-start.5
  59.0 16.6 %collective-permute-start = (bf16[2,1024,128]{2,1,0:T(8,128)(2,1)}, bf16[2,1024,128]{2,1,0:T(8,128)(2,1)}, u32[]{:S(2)}, u32[]{:S(2)}) collective-permute-start(bf16[2,1024,128]{2,1,0:T(8,128)(2,1)} %pad_maximum_fusion), channel_id=1, source_target_pairs={{0,2},{1,3},{2,4},{3,5},{4,6},{5,7},{6,8},{7,9},{8,10},{9,11},{10,... | collective-permute-start | bytes 1572872 | tf_op jit(solution)/shard_map/ppermute | solution.py:293
  74.6 1.0 copy-start.1
  75.6 9.2 %copy-start.7 = (bf16[1,1024,128]{2,1,0:T(8,128)(2,1)S(1)}, bf16[1,1024,128]{2,1,0:T(8,128)(2,1)}, u32[]{:S(2)}) copy-start(bf16[1,1024,128]{2,1,0:T(8,128)(2,1)} %param.12) | copy-start | bytes 786436
  75.6 9.2 %copy-start.8 = (bf16[1,1024,128]{2,1,0:T(8,128)(2,1)S(1)}, bf16[1,1024,128]{2,1,0:T(8,128)(2,1)}, u32[]{:S(2)}) copy-start(bf16[1,1024,128]{2,1,0:T(8,128)(2,1)} %param.13) | copy-start | bytes 786436
  75.6 9.2 %copy-start.11 = (bf16[1,1024,128]{2,1,0:T(8,128)(2,1)S(1)}, bf16[1,1024,128]{2,1,0:T(8,128)(2,1)}, u32[]{:S(2)}) copy-start(bf16[1,1024,128]{2,1,0:T(8,128)(2,1)} %param.11) | copy-start | bytes 786436
  75.6 22.9 %all-to-all-start.1 = ((bf16[32,128,128]{2,1,0:T(8,128)(2,1)}), bf16[32,128,128]{2,1,0:T(8,128)(2,1)S(1)}, u32[]{:S(2)}, u32[]{:S(2)}) async-start(bf16[32,128,128]{2,1,0:T(8,128)(2,1)} %copy-done.1), calls=%async_computation.1 | async-start | bytes 2097152 | tf_op jit(solution)/shard_map/all_to_all | solution.py:307
  81.6 16.9 %copy-start.6 = (bf16[1024,128]{1,0:T(8,128)(2,1)S(1)}, bf16[1024,128]{1,0:T(8,128)(2,1)}, u32[]{:S(2)}) copy-start(bf16[1024,128]{1,0:T(8,128)(2,1)} %copy-done.5) | copy-start | bytes 786436
  82.7 2.0 %collective-permute-start.1 = (bf16[2,1024,128]{2,1,0:T(8,128)(2,1)S(1)}, bf16[2,1024,128]{2,1,0:T(8,128)(2,1)S(1)}, u32[]{:S(2)}, u32[]{:S(2)}) collective-permute-start(bf16[2,1024,128]{2,1,0:T(8,128)(2,1)S(1)} %broadcast_select_fusion), channel_id=1, source_target_pairs={{0,1},{1,0},{2,3},{3,2},{4,5},{5,4},{6,7},{7,6},{8,9},{9,8},{10,11... | collective-permute-start | bytes 1572872 | tf_op jit(solution)/shard_map/ppermute | solution.py:309

commit v4 on v3

--- a/solution.py
+++ b/solution.py
@@ -17,20 +17,48 @@
 EMPTY = 256.0
 GROUP = 8
 CHUNK = 1024
+SENDS = (0, 24, 32)
 VMEM = pl.BlockSpec(memory_space=pltpu.VMEM)
+HBM = pl.BlockSpec(memory_space=pltpu.HBM)
 
 
 def in_vmem(array):
     return pltpu.with_memory_space_constraint(array, pltpu.VMEM)
 
 
+def in_hbm(array):
+    return pltpu.with_memory_space_constraint(array, pltpu.HBM)
+
+
 def params():
     return pltpu.CompilerParams(vmem_limit_bytes=40 * 1024 * 1024)
 
 
-def pack_kernel(ids_ref, q_ref, k_ref, v_ref, sent_ref, rank_ref):
+def pack_kernel(
+    ids_ref,
+    q_ref,
+    k_ref,
+    v_ref,
+    sent_ref,
+    place_ref,
+    start_ref,
+    rows_ref,
+    sorted_ref,
+    stage_ref,
+    start_smem,
+    in_sems,
+    out_sems,
+    start_sem,
+):
+    loads = [
+        pltpu.make_async_copy(ref, rows_ref.at[i], in_sems.at[i])
+        for i, ref in enumerate((q_ref, k_ref, v_ref))
+    ]
+    for load in loads:
+        load.start()
     ids = ids_ref[...]
-    member = (ids == lax.broadcasted_iota(jnp.int32, (CLUSTERS, TOK), 0)).astype(jnp.float32)
+    cluster = lax.broadcasted_iota(jnp.int32, (CLUSTERS, TOK), 0)
+    member = (ids == cluster).astype(jnp.float32)
     member_b = member.astype(jnp.bfloat16)
     upto = (
         lax.broadcasted_iota(jnp.int32, (128, 128), 0)
@@ -46,41 +74,80 @@
             jnp.sum(member[:, first : first + 128] * seen, axis=0, keepdims=True) - 1.0
         )
         count = seen[:, 127:128]
-    rank = jnp.concatenate(ranks, axis=1)
-    rank_ref[...] = jnp.broadcast_to(rank, rank_ref.shape)
-    at_rank = (
-        rank.astype(jnp.int32) == lax.broadcasted_iota(jnp.int32, (CAP, TOK), 0)
-    ).astype(jnp.bfloat16)
-    rows = jnp.concatenate([q_ref[...], k_ref[...], v_ref[...]], axis=1)
-    slot = lax.broadcasted_iota(jnp.int32, (CAP, D), 0).astype(jnp.float32)
+    line = lax.broadcasted_iota(jnp.int32, (CLUSTERS, 128), 0)
+    lane = lax.broadcasted_iota(jnp.int32, (CLUSTERS, 128), 1)
+    start = jnp.sum(
+        jnp.where(line < lane, jnp.broadcast_to(count, (CLUSTERS, 128)), 0.0),
+        axis=0,
+        keepdims=True,
+    )
+    start_ref[...] = jnp.broadcast_to(start, start_ref.shape).astype(jnp.int32)
+    starts = pltpu.make_async_copy(start_ref, start_smem, start_sem)
+    starts.start()
+    before = jnp.sum(
+        jnp.where(cluster < ids, jnp.broadcast_to(count, (CLUSTERS, TOK)), 0.0),
+        axis=0,
+        keepdims=True,
+    )
+    place = before + jnp.concatenate(ranks, axis=1)
+    place_ref[...] = jnp.broadcast_to(place, place_ref.shape)
+    place = place.astype(jnp.int32)
+    for load in loads:
+        load.wait()
+    rows = jnp.concatenate([rows_ref[i] for i in range(3)], axis=1)
+    size = 256
+    for low in range(0, TOK, size):
+        line = lax.broadcasted_iota(jnp.int32, (size, TOK), 0) + low
+        in_order = jnp.dot(
+            (place == line).astype(jnp.float32).astype(jnp.bfloat16),
+            rows,
+            preferred_element_type=jnp.float32,
+        )
+        for i in range(3):
+            sorted_ref[i, low : low + size] = in_order[:, i * D : (i + 1) * D]
+    starts.wait()
+    slot = lax.broadcasted_iota(jnp.int32, (CAP, D), 0)
+    sends = []
     for base in range(0, CLUSTERS, GROUP):
-        place = jnp.concatenate(
-            [at_rank * member_b[c : c + 1] for c in range(base, base + GROUP)], axis=0
-        )
-        placed = jnp.dot(place, rows, preferred_element_type=jnp.float32)
-        for i in range(GROUP):
-            c = base + i
-            mine = placed[i * CAP : (i + 1) * CAP]
-            sent_ref[c, 0:CAP] = mine[:, 0:D].astype(jnp.bfloat16)
-            used = slot < jnp.broadcast_to(count[c : c + 1], (CAP, D))
-            sent_ref[c, CAP : 2 * CAP] = jnp.where(used, mine[:, D : 2 * D], EMPTY).astype(
-                jnp.bfloat16
+        for c in range(base, base + GROUP):
+            first = start_smem[0, c]
+            used = slot < start_smem[0, c + 1] - first
+            for i, blank in enumerate((0.0, EMPTY, 0.0)):
+                mine = jnp.where(used, sorted_ref[i, pl.ds(first, CAP)], blank)
+                stage_ref[c, i * CAP : (i + 1) * CAP] = mine.astype(jnp.bfloat16)
+        part = pl.ds(base, GROUP)
+        sends.append(
+            pltpu.make_async_copy(
+                stage_ref.at[part], sent_ref.at[part], out_sems.at[base // GROUP]
             )
-            sent_ref[c, 2 * CAP : 3 * CAP] = mine[:, 2 * D : 3 * D].astype(jnp.bfloat16)
+        )
+        sends[-1].start()
+    for send in sends:
+        send.wait()
 
 
 def pack(ids, q, k, v):
     return pl.pallas_call(
         pack_kernel,
         out_shape=(
-            jax.ShapeDtypeStruct((CLUSTERS, 3 * CAP, D), jnp.bfloat16),
+            pltpu.HBM((CLUSTERS, 3 * CAP, D), jnp.bfloat16),
             pltpu.VMEM((8, TOK), jnp.float32),
+            pltpu.VMEM((8, 128), jnp.int32),
         ),
-        in_specs=[VMEM] * 4,
-        out_specs=(VMEM, VMEM),
+        in_specs=[VMEM] + [HBM] * 3,
+        out_specs=(HBM, VMEM, VMEM),
+        scratch_shapes=[
+            pltpu.VMEM((3, TOK, D), jnp.bfloat16),
+            pltpu.VMEM((3, TOK + CAP, D), jnp.float32),
+            pltpu.VMEM((CLUSTERS, 3 * CAP, D), jnp.bfloat16),
+            pltpu.SMEM((8, 128), jnp.int32),
+            pltpu.SemaphoreType.DMA((3,)),
+            pltpu.SemaphoreType.DMA((CLUSTERS // GROUP,)),
+            pltpu.SemaphoreType.DMA,
+        ],
         compiler_params=params(),
         name="pack_slots",
-    )(ids, q, k, v)
+    )(ids, in_hbm(q), in_hbm(k), in_hbm(v))
 
 
 def attend(tasks, query_of, key_ref, value_ref, write):
@@ -121,41 +188,55 @@
     ]
 
 
-def routed_kernel(got_ref, out_ref, key_ref, value_ref):
+def routed_kernel(
+    got_ref,
+    out_ref,
+    key_ref,
+    value_ref,
+    mixed_ref,
+    out_sems,
+):
     blocks = got_ref.shape[0]
     first = jnp.zeros((1, D), jnp.float32)
     for s in reversed(range(blocks)):
         row = got_ref[s, CAP : CAP + 16].astype(jnp.float32)[0:1]
         first = jnp.where(row < 100.0, row, first)
     filler = jnp.broadcast_to(first, (CAP, D))
-    for s in range(blocks):
-        key = got_ref[s, CAP : 2 * CAP].astype(jnp.float32)
-        used = key < 100.0
-        key_ref[s * CAP : (s + 1) * CAP] = jnp.where(used, key, filler).astype(jnp.bfloat16)
-        value_ref[s * CAP : (s + 1) * CAP, 0:D] = got_ref[s, 2 * CAP : 3 * CAP]
-        value_ref[s * CAP : (s + 1) * CAP, D : 2 * D] = used.astype(jnp.float32).astype(
-            jnp.bfloat16
-        )
     size = 2 * CAP
     within = lax.broadcasted_iota(jnp.int32, (size, size), 1) <= lax.broadcasted_iota(
         jnp.int32, (size, size), 0
     )
+    for s in range(blocks):
+        at = slice(s * CAP, (s + 1) * CAP)
+        key = got_ref[s, CAP : 2 * CAP].astype(jnp.float32)
+        used = key < 100.0
+        key_ref[at] = jnp.where(used, key, filler).astype(jnp.bfloat16)
+        value_ref[at, 0:D] = got_ref[s, 2 * CAP : 3 * CAP]
+        value_ref[at, D : 2 * D] = used.astype(jnp.float32).astype(jnp.bfloat16)
+
+    def query_of(i):
+        return got_ref[2 * i : 2 * i + 2, 0:CAP].reshape(size, D)
+
     tasks = []
     for i in range(blocks // 2):
         own = i * size
         spans = [(low, min(low + CHUNK, own), None) for low in range(0, own, CHUNK)]
         tasks += tasks_of(i, spans + [(own, own + size, within)])
+    sends = []
 
     def write(i, mixed):
-        out_ref[2 * i : 2 * i + 2] = mixed.reshape(2, CAP, D)
-
-    attend(
-        tasks,
-        lambda i: got_ref[2 * i : 2 * i + 2, 0:CAP].reshape(size, D),
-        key_ref,
-        value_ref,
-        write,
-    )
+        mixed_ref[2 * i : 2 * i + 2] = mixed.reshape(2, CAP, D)
+        if 2 * i + 2 in SENDS:
+            n = SENDS.index(2 * i + 2)
+            part = pl.ds(SENDS[n - 1], SENDS[n] - SENDS[n - 1])
+            sends.append(
+                pltpu.make_async_copy(mixed_ref.at[part], out_ref.at[part], out_sems.at[n - 1])
+            )
+            sends[-1].start()
+
+    attend(tasks, query_of, key_ref, value_ref, write)
+    for send in sends:
+        send.wait()
 
 
 def routed(got):
@@ -163,12 +244,14 @@
     slots = blocks * CAP
     return pl.pallas_call(
         routed_kernel,
-        out_shape=jax.ShapeDtypeStruct((blocks, CAP, D), jnp.bfloat16),
+        out_shape=pltpu.HBM((blocks, CAP, D), jnp.bfloat16),
         in_specs=[VMEM],
-        out_specs=VMEM,
+        out_specs=HBM,
         scratch_shapes=[
             pltpu.VMEM((slots, D), jnp.bfloat16),
             pltpu.VMEM((slots, 2 * D), jnp.bfloat16),
+            pltpu.VMEM((blocks, CAP, D), jnp.bfloat16),
+            pltpu.SemaphoreType.DMA((len(SENDS) - 1,)),
         ],
         compiler_params=params(),
         cost_estimate=pl.CostEstimate(
@@ -240,52 +323,44 @@
     )(at, q, k, v, in_vmem(far), in_vmem(near))
 
 
-def slot_kernel(ids_ref, rank_ref, at_rank_ref, ids_col_ref):
-    rank = jnp.broadcast_to(rank_ref[0:1], (D, TOK)).T
-    lane = lax.broadcasted_iota(jnp.int32, (TOK, CAP), 1)
-    at_rank_ref[...] = (rank.astype(jnp.int32) == lane).astype(jnp.bfloat16)
-    ids = jnp.broadcast_to(ids_ref[...].astype(jnp.float32), (D, TOK)).T
-    ids_col_ref[...] = ids.astype(jnp.bfloat16)
-
-
-def slots(ids, rank):
+def pick_kernel(place_ref, pick_ref):
+    place = jnp.broadcast_to(place_ref[0:1], (128, TOK)).T.astype(jnp.int32)
+    lane = lax.broadcasted_iota(jnp.int32, (TOK, 128), 1)
+    for low in range(0, TOK, 128):
+        pick_ref[:, low : low + 128] = (
+            (place == lane + low).astype(jnp.float32).astype(jnp.bfloat16)
+        )
+
+
+def picks(place):
     return pl.pallas_call(
-        slot_kernel,
-        out_shape=(
-            pltpu.VMEM((TOK, CAP), jnp.bfloat16),
-            pltpu.VMEM((TOK, CAP), jnp.bfloat16),
-        ),
-        in_specs=[VMEM] * 2,
-        out_specs=(VMEM, VMEM),
+        pick_kernel,
+        out_shape=pltpu.VMEM((TOK, TOK), jnp.bfloat16),
+        in_specs=[VMEM],
+        out_specs=VMEM,
         compiler_params=params(),
-        name="slot_columns",
-    )(ids, in_vmem(rank))
-
-
-def unpack_kernel(at_rank_ref, ids_ref, back_ref, out_ref):
-    rows = 256
-    for low in range(0, TOK, rows):
-        at_rank = at_rank_ref[low : low + rows]
-        ids = ids_ref[low : low + rows]
-        zero = jnp.zeros_like(at_rank)
-        picks = [
-            jnp.where(ids == jnp.asarray(c, jnp.bfloat16), at_rank, zero) for c in range(CLUSTERS)
-        ]
-        pick = jnp.concatenate(picks, axis=1)
-        out_ref[low : low + rows] = jnp.dot(
-            pick, back_ref[...], preferred_element_type=jnp.float32
-        ).astype(jnp.bfloat16)
-
-
-def unpack(at_rank, ids_col, back):
+        name="picks",
+    )(in_vmem(place))
+
+
+def unpack_kernel(start_ref, pick_ref, back_ref, out_ref, sorted_ref):
+    for c in range(CLUSTERS):
+        sorted_ref[pl.ds(start_ref[0, c], CAP)] = back_ref[c].astype(jnp.float32)
+    out_ref[...] = jnp.dot(
+        pick_ref[...], sorted_ref[0:TOK].astype(jnp.bfloat16), preferred_element_type=jnp.float32
+    ).astype(jnp.bfloat16)
+
+
+def unpack(start, pick, back):
     return pl.pallas_call(
         unpack_kernel,
         out_shape=jax.ShapeDtypeStruct((TOK, D), jnp.bfloat16),
-        in_specs=[VMEM] * 3,
+        in_specs=[pl.BlockSpec(memory_space=pltpu.SMEM), VMEM, VMEM],
         out_specs=VMEM,
+        scratch_shapes=[pltpu.VMEM((TOK + CAP, D), jnp.float32)],
         compiler_params=params(),
         name="unpack_slots",
-    )(in_vmem(at_rank), in_vmem(ids_col), in_vmem(back))
+    )(start, in_vmem(pick), in_vmem(back))
 
 
 def passed_along(value, steps):
@@ -296,14 +371,14 @@
 def local(q_routed, k_routed, v_routed, memberships, q_local, k_local, v_local):
     seq_index = lax.axis_index(SEQ)
     ids = memberships.reshape(1, TOK)
-    sent, rank = pack(ids, q_routed[0], k_routed[0], v_routed[0])
+    sent, place, start = pack(ids, q_routed[0], k_routed[0], v_routed[0])
     got = lax.all_to_all(sent, SEQ, split_axis=0, concat_axis=0, tiled=True)
     pair = jnp.concatenate([k_local, v_local], axis=0)
-    at_rank, ids_col = slots(ids, rank)
-    got, pair, at_rank, ids_col = lax.optimization_barrier((got, pair, at_rank, ids_col))
+    got, pair = lax.optimization_barrier((got, pair))
     far = passed_along(pair, 2)
     mixed = routed(got)
-    mixed, far = lax.optimization_barrier((mixed, far))
+    mixed, far, place = lax.optimization_barrier((mixed, far, place))
+    pick = picks(place)
     back = lax.all_to_all(mixed, SEQ, split_axis=0, concat_axis=0, tiled=True)
     given = jnp.where(seq_index % 2 == 1, far, pair)
     near = lax.ppermute(given, SEQ, [(s, s ^ 1) for s in range(lax.axis_size(SEQ))])
@@ -311,7 +386,7 @@
         seq_index.astype(jnp.int32).reshape(1), q_local[0], k_local[0], v_local[0], far, near
     )
     back, out_local = lax.optimization_barrier((back, out_local))
-    out_routed = unpack(at_rank, ids_col, back.reshape(CLUSTERS * CAP, D))
+    out_routed = unpack(start, pick, back)
     return (out_routed[None], out_local[None])
 
 

time: 102 us -> 95.8 us (0.939)
  local copies, waits for them, and re-layouts: 6.85 us -> 2.59 us
  waiting for transfers between devices: 47 us -> 45.7 us
    unnamed x24 -> x8, local copies, waits for them, and re-layouts: 6.85 us -> 2.59 us
    all_to_all x1, waiting for transfers between devices: 8.44 us -> 6.56 us  [local(): back = lax.all_to_all(mixed, SEQ, split_axis=0, concat_axis=0, tiled=True)]
    all_to_all x1, waiting for transfers between devices: 36.9 us -> 37.9 us  [local(): got = lax.all_to_all(sent, SEQ, split_axis=0, concat_axis=0, tiled=True)]
  transfers between devices with their start and end apart: 4 -> 4, of which waited for: 3 -> 3; matrix products, arithmetic and copies ran while one was open for 3% -> 3% of each run, Pallas kernels for 18% -> 20%
where the time goes in v4:
time: 95.8 us; the launch traced here: 95.3 us
  waiting for transfers between devices  45.7 us (48%)
  Pallas kernels  25.2 us (26%)
  starting transfers between devices  18.2 us (19%)
  other arithmetic  2.92 us (3%)
  local copies, waits for them, and re-layouts  2.59 us (3%)
    all_to_all x1, waiting for transfers between devices, local(): got = lax.all_to_all(sent, SEQ, split_axis=0, concat_axis=0, tiled=True)  37.9 us
    pallas_call x1, Pallas kernels, routed(): pl.pallas_call(routed_kernel, out_shape=pltpu.HBM((blocks, CAP, D), jnp.b...  13 us
    all_to_all x1, starting transfers between devices, local(): got = lax.all_to_all(sent, SEQ, split_axis=0, concat_axis=0, tiled=True)  8.73 us
    all_to_all x1, waiting for transfers between devices, local(): back = lax.all_to_all(mixed, SEQ, split_axis=0, concat_axis=0, tiled=True)  6.56 us
    all_to_all x1, starting transfers between devices, local(): back = lax.all_to_all(mixed, SEQ, split_axis=0, concat_axis=0, tiled=True)  5.8 us
    pallas_call x1, Pallas kernels, windowed(): pl.pallas_call(local_kernel, out_shape=jax.ShapeDtypeStruct((TOK, D), jnp...  5.32 us
    pallas_call x1, Pallas kernels, pack(): pl.pallas_call(pack_kernel, out_shape=(pltpu.HBM((CLUSTERS, 3 * CAP, D),...  4.2 us
    ppermute x1, starting transfers between devices, passed_along(): lax.ppermute(value, SEQ, [(s, s + steps) for s in range(count - steps)])  3.35 us
  transfers between devices with their start and end apart: 4, of which 3 were waited for; matrix products, arithmetic and copies ran while one was open for 3% of the time, Pallas kernels for 20%

profile of v4, /device:TPU:1, one launch (start us, length us, event | category | flops | bytes accessed | tf_op | source)
XLA Modules:
  0.0 95.3 jit_solution(120716553175412813)
XLA Ops:
  0.6 0.0 copy-start.2
  0.6 0.7 copy-done.2
  1.3 4.2 %pack_slots.1 = (bf16[32,384,128]{2,1,0:T(8,128)(2,1)}, f32[8,1024]{1,0:T(8,128)S(1)}, s32[8,128]{1,0:T(8,128)S(1)}) custom-call(s32[1,1024]{1,0:T(1,128)S(1)} %bitcast.12, bf16[1024,128]{1,0:T(8,128)(2,1)} %bitcast.14, bf16[1024,128]{1,0:T(8,128)(2,1)} %bitcast.15, bf16[1024,128]{1,0:T(8,128)(2,1)} %bitcast.16), custom_call_target="tpu_custom_call" | custom-call | tf_op jit(solution)/shard_map/pack_slots/pallas_call | solution.py:130
  5.5 0.0 copy-start
  5.5 8.7 %all-to-all-start = ((bf16[32,384,128]{2,1,0:T(8,128)(2,1)}), bf16[32,384,128]{2,1,0:T(8,128)(2,1)S(1)}, u32[]{:S(2)}, u32[]{:S(2)}) async-start(bf16[32,384,128]{2,1,0:T(8,128)(2,1)} %get-tuple-element.13), calls=%async_computation | async-start | bytes 6291456 | tf_op jit(solution)/shard_map/all_to_all | solution.py:375
  14.3 0.0 copy-done
  14.3 1.8 %pad_maximum_fusion = bf16[2,1024,128]{2,1,0:T(8,128)(2,1)} fusion(bf16[1,1024,128]{2,1,0:T(8,128)(2,1)} %param.13, bf16[1,1024,128]{2,1,0:T(8,128)(2,1)S(1)} %copy-done), kind=kLoop, calls=%fused_computation | loop fusion | flops 262144 | bytes 1048576 | tf_op jit(solution)/shard_map/concatenate | solution.py:376
  16.1 37.9 %all-to-all-done.got_ref = bf16[32,384,128]{2,1,0:T(8,128)(2,1)S(1)} async-done(((bf16[32,384,128]{2,1,0:T(8,128)(2,1)}), bf16[32,384,128]{2,1,0:T(8,128)(2,1)S(1)}, u32[]{:S(2)}, u32[]{:S(2)}) %all-to-all-start) | async-done | bytes 3145760 | tf_op jit(solution)/shard_map/all_to_all | solution.py:375
  54.0 3.4 %collective-permute-start = (bf16[2,1024,128]{2,1,0:T(8,128)(2,1)}, bf16[2,1024,128]{2,1,0:T(8,128)(2,1)}, u32[]{:S(2)}, u32[]{:S(2)}) collective-permute-start(bf16[2,1024,128]{2,1,0:T(8,128)(2,1)} %pad_maximum_fusion), channel_id=1, source_target_pairs={{0,2},{1,3},{2,4},{3,5},{4,6},{5,7},{6,8},{7,9},{8,10},{9,11},{10,... | collective-permute-start | bytes 1572872 | tf_op jit(solution)/shard_map/ppermute | solution.py:368
  57.4 13.0 %cluster_attention.1 = bf16[32,128,128]{2,1,0:T(8,128)(2,1)} custom-call(bf16[32,384,128]{2,1,0:T(8,128)(2,1)S(1)} %all-to-all-done.got_ref), custom_call_target="tpu_custom_call" | custom-call | flops 8589934592 | bytes 4194304 | tf_op jit(solution)/shard_map/cluster_attention/pallas_call | solution.py:245
  70.4 0.0 collective-permute-done.far_ref
  70.4 5.8 %all-to-all-start.1 = ((bf16[32,128,128]{2,1,0:T(8,128)(2,1)}), bf16[32,128,128]{2,1,0:T(8,128)(2,1)S(1)}, u32[]{:S(2)}, u32[]{:S(2)}) async-start(bf16[32,128,128]{2,1,0:T(8,128)(2,1)} %cluster_attention.1), calls=%async_computation.1 | async-start | bytes 2097152 | tf_op jit(solution)/shard_map/all_to_all | solution.py:382
  76.2 1.1 %broadcast_select_fusion = bf16[2,1024,128]{2,1,0:T(8,128)(2,1)S(1)} fusion(bf16[2,1024,128]{2,1,0:T(8,128)(2,1)} %collective-permute-done.far_ref, bf16[2,1024,128]{2,1,0:T(8,128)(2,1)} %pad_maximum_fusion, pred[]{:T(512)S(6)} %eq.5), kind=kLoop, calls=%fused_computation.1 | loop fusion | flops 262144 | bytes 1572865 | tf_op jit(solution)/shard_map/jit(_where)/select_n | solution.py:383
  77.4 0.3 collective-permute-start.1
  77.7 0.5 picks.1.pick_ref
  78.2 1.2 %collective-permute-done.1.near_ref = bf16[2,1024,128]{2,1,0:T(8,128)(2,1)S(1)} collective-permute-done((bf16[2,1024,128]{2,1,0:T(8,128)(2,1)S(1)}, bf16[2,1024,128]{2,1,0:T(8,128)(2,1)S(1)}, u32[]{:S(2)}, u32[]{:S(2)}) %collective-permute-start.1) | collective-permute-done | bytes 524320 | tf_op jit(solution)/shard_map/ppermute | solution.py:384
  79.3 0.0 copy-start.1
  79.4 0.9 copy-done.1
  80.3 0.0 copy-start.3
  80.3 0.9 copy-done.3
  81.3 5.3 %window_attention.1 = bf16[1024,128]{1,0:T(8,128)(2,1)} custom-call(s32[1]{0:T(128)} %bitcast.4.at_ref, bf16[1024,128]{1,0:T(8,128)(2,1)S(1)} %bitcast.13, bf16[1024,128]{1,0:T(8,128)(2,1)S(1)} %bitcast.10, bf16[1024,128]{1,0:T(8,128)(2,1)S(1)} %bitcast.11, bf16[2,1024,128]{2,1,0:T(8,128)(2,1)} %collective-permute-done.far_ref, ...), custom_call_target="tpu_custom_call" | custom-call | flops 1207959552 | bytes 2097152 | tf_op jit(solution)/shard_map/window_attention/pallas_call | solution.py:309
  86.6 6.6 %all-to-all-done.1.back_ref = bf16[32,128,128]{2,1,0:T(8,128)(2,1)S(1)} async-done(((bf16[32,128,128]{2,1,0:T(8,128)(2,1)}), bf16[32,128,128]{2,1,0:T(8,128)(2,1)S(1)}, u32[]{:S(2)}, u32[]{:S(2)}) %all-to-all-start.1) | async-done | bytes 1048608 | tf_op jit(solution)/shard_map/all_to_all | solution.py:382
  93.1 2.1 %unpack_slots.1 = bf16[1024,128]{1,0:T(8,128)(2,1)} custom-call(s32[8,128]{1,0:T(8,128)S(1)} %get-tuple-element.12.start_ref, bf16[1024,1024]{1,0:T(8,128)(2,1)S(1)} %picks.1.pick_ref, bf16[32,128,128]{2,1,0:T(8,128)(2,1)S(1)} %all-to-all-done.1.back_ref), custom_call_target="tpu_custom_call" | custom-call | tf_op jit(solution)/shard_map/unpack_slots/pallas_call | solution.py:355
Async XLA Ops:
  0.6 0.7 copy-start.2
  5.5 8.8 %copy-start = (bf16[1,1024,128]{2,1,0:T(8,128)(2,1)S(1)}, bf16[1,1024,128]{2,1,0:T(8,128)(2,1)}, u32[]{:S(2)}) copy-start(bf16[1,1024,128]{2,1,0:T(8,128)(2,1)} %param.12) | copy-start | bytes 786436
  5.5 48.5 %all-to-all-start = ((bf16[32,384,128]{2,1,0:T(8,128)(2,1)}), bf16[32,384,128]{2,1,0:T(8,128)(2,1)S(1)}, u32[]{:S(2)}, u32[]{:S(2)}) async-start(bf16[32,384,128]{2,1,0:T(8,128)(2,1)} %get-tuple-element.13), calls=%async_computation | async-start | bytes 6291456 | tf_op jit(solution)/shard_map/all_to_all | solution.py:375
  54.0 16.4 %collective-permute-start = (bf16[2,1024,128]{2,1,0:T(8,128)(2,1)}, bf16[2,1024,128]{2,1,0:T(8,128)(2,1)}, u32[]{:S(2)}, u32[]{:S(2)}) collective-permute-start(bf16[2,1024,128]{2,1,0:T(8,128)(2,1)} %pad_maximum_fusion), channel_id=1, source_target_pairs={{0,2},{1,3},{2,4},{3,5},{4,6},{5,7},{6,8},{7,9},{8,10},{9,11},{10,... | collective-permute-start | bytes 1572872 | tf_op jit(solution)/shard_map/ppermute | solution.py:368
  70.4 22.7 %all-to-all-start.1 = ((bf16[32,128,128]{2,1,0:T(8,128)(2,1)}), bf16[32,128,128]{2,1,0:T(8,128)(2,1)S(1)}, u32[]{:S(2)}, u32[]{:S(2)}) async-start(bf16[32,128,128]{2,1,0:T(8,128)(2,1)} %cluster_attention.1), calls=%async_computation.1 | async-start | bytes 2097152 | tf_op jit(solution)/shard_map/all_to_all | solution.py:382
  77.4 2.0 %collective-permute-start.1 = (bf16[2,1024,128]{2,1,0:T(8,128)(2,1)S(1)}, bf16[2,1024,128]{2,1,0:T(8,128)(2,1)S(1)}, u32[]{:S(2)}, u32[]{:S(2)}) collective-permute-start(bf16[2,1024,128]{2,1,0:T(8,128)(2,1)S(1)} %broadcast_select_fusion), channel_id=1, source_target_pairs={{0,1},{1,0},{2,3},{3,2},{4,5},{5,4},{6,7},{7,6},{8,9},{9,8},{10,11... | collective-permute-start | bytes 1572872 | tf_op jit(solution)/shard_map/ppermute | solution.py:384
  79.3 1.0 copy-start.1
  80.3 0.9 copy-start.3

commit v5 on v4

--- a/solution.py
+++ b/solution.py
@@ -377,8 +377,9 @@
     got, pair = lax.optimization_barrier((got, pair))
     far = passed_along(pair, 2)
     mixed = routed(got)
-    mixed, far, place = lax.optimization_barrier((mixed, far, place))
+    mixed, place = lax.optimization_barrier((mixed, place))
     pick = picks(place)
+    far, pick = lax.optimization_barrier((far, pick))
     back = lax.all_to_all(mixed, SEQ, split_axis=0, concat_axis=0, tiled=True)
     given = jnp.where(seq_index % 2 == 1, far, pair)
     near = lax.ppermute(given, SEQ, [(s, s ^ 1) for s in range(lax.axis_size(SEQ))])

time: 95.8 us -> 95.8 us (level)
  no operation moved by 1% of the time
where the time goes in v5:
time: 95.8 us; the launch traced here: 95.3 us
  waiting for transfers between devices  45.6 us (48%)
  Pallas kernels  25.2 us (26%)
  starting transfers between devices  18.2 us (19%)
  other arithmetic  2.92 us (3%)
  local copies, waits for them, and re-layouts  2.59 us (3%)
    all_to_all x1, waiting for transfers between devices, local(): got = lax.all_to_all(sent, SEQ, split_axis=0, concat_axis=0, tiled=True)  37.9 us
    pallas_call x1, Pallas kernels, routed(): pl.pallas_call(routed_kernel, out_shape=pltpu.HBM((blocks, CAP, D), jnp.b...  13 us
    all_to_all x1, starting transfers between devices, local(): got = lax.all_to_all(sent, SEQ, split_axis=0, concat_axis=0, tiled=True)  8.73 us
    all_to_all x1, waiting for transfers between devices, local(): back = lax.all_to_all(mixed, SEQ, split_axis=0, concat_axis=0, tiled=True)  6.03 us
    all_to_all x1, starting transfers between devices, local(): back = lax.all_to_all(mixed, SEQ, split_axis=0, concat_axis=0, tiled=True)  5.8 us
    pallas_call x1, Pallas kernels, windowed(): pl.pallas_call(local_kernel, out_shape=jax.ShapeDtypeStruct((TOK, D), jnp...  5.33 us
    pallas_call x1, Pallas kernels, pack(): pl.pallas_call(pack_kernel, out_shape=(pltpu.HBM((CLUSTERS, 3 * CAP, D),...  4.2 us
    ppermute x1, starting transfers between devices, passed_along(): lax.ppermute(value, SEQ, [(s, s + steps) for s in range(count - steps)])  3.35 us
  transfers between devices with their start and end apart: 4, of which 3 were waited for; matrix products, arithmetic and copies ran while one was open for 3% of the time, Pallas kernels for 20%

profile of v5, /device:TPU:1, one launch (start us, length us, event | category | flops | bytes accessed | tf_op | source)
XLA Modules:
  0.0 95.3 jit_solution(16428324331683838935)
XLA Ops:
  0.6 0.0 copy-start.2
  0.6 0.7 copy-done.2
  1.3 4.2 %pack_slots.1 = (bf16[32,384,128]{2,1,0:T(8,128)(2,1)}, f32[8,1024]{1,0:T(8,128)S(1)}, s32[8,128]{1,0:T(8,128)S(1)}) custom-call(s32[1,1024]{1,0:T(1,128)S(1)} %bitcast.12, bf16[1024,128]{1,0:T(8,128)(2,1)} %bitcast.14, bf16[1024,128]{1,0:T(8,128)(2,1)} %bitcast.15, bf16[1024,128]{1,0:T(8,128)(2,1)} %bitcast.16), custom_call_target="tpu_custom_call" | custom-call | tf_op jit(solution)/shard_map/pack_slots/pallas_call | solution.py:130
  5.5 0.0 copy-start
  5.5 8.7 %all-to-all-start = ((bf16[32,384,128]{2,1,0:T(8,128)(2,1)}), bf16[32,384,128]{2,1,0:T(8,128)(2,1)S(1)}, u32[]{:S(2)}, u32[]{:S(2)}) async-start(bf16[32,384,128]{2,1,0:T(8,128)(2,1)} %get-tuple-element.14), calls=%async_computation | async-start | bytes 6291456 | tf_op jit(solution)/shard_map/all_to_all | solution.py:375
  14.3 0.0 copy-done
  14.3 1.8 %pad_maximum_fusion = bf16[2,1024,128]{2,1,0:T(8,128)(2,1)} fusion(bf16[1,1024,128]{2,1,0:T(8,128)(2,1)} %param.13, bf16[1,1024,128]{2,1,0:T(8,128)(2,1)S(1)} %copy-done), kind=kLoop, calls=%fused_computation | loop fusion | flops 262144 | bytes 1048576 | tf_op jit(solution)/shard_map/concatenate | solution.py:376
  16.1 37.9 %all-to-all-done.got_ref = bf16[32,384,128]{2,1,0:T(8,128)(2,1)S(1)} async-done(((bf16[32,384,128]{2,1,0:T(8,128)(2,1)}), bf16[32,384,128]{2,1,0:T(8,128)(2,1)S(1)}, u32[]{:S(2)}, u32[]{:S(2)}) %all-to-all-start) | async-done | bytes 3145760 | tf_op jit(solution)/shard_map/all_to_all | solution.py:375
  54.0 3.4 %collective-permute-start = (bf16[2,1024,128]{2,1,0:T(8,128)(2,1)}, bf16[2,1024,128]{2,1,0:T(8,128)(2,1)}, u32[]{:S(2)}, u32[]{:S(2)}) collective-permute-start(bf16[2,1024,128]{2,1,0:T(8,128)(2,1)} %pad_maximum_fusion), channel_id=1, source_target_pairs={{0,2},{1,3},{2,4},{3,5},{4,6},{5,7},{6,8},{7,9},{8,10},{9,11},{10,... | collective-permute-start | bytes 1572872 | tf_op jit(solution)/shard_map/ppermute | solution.py:368
  57.4 13.0 %cluster_attention.1 = bf16[32,128,128]{2,1,0:T(8,128)(2,1)} custom-call(bf16[32,384,128]{2,1,0:T(8,128)(2,1)S(1)} %all-to-all-done.got_ref), custom_call_target="tpu_custom_call" | custom-call | flops 8589934592 | bytes 4194304 | tf_op jit(solution)/shard_map/cluster_attention/pallas_call | solution.py:245
  70.4 5.8 %all-to-all-start.1 = ((bf16[32,128,128]{2,1,0:T(8,128)(2,1)}), bf16[32,128,128]{2,1,0:T(8,128)(2,1)S(1)}, u32[]{:S(2)}, u32[]{:S(2)}) async-start(bf16[32,128,128]{2,1,0:T(8,128)(2,1)} %cluster_attention.1), calls=%async_computation.1 | async-start | bytes 2097152 | tf_op jit(solution)/shard_map/all_to_all | solution.py:383
  76.2 0.5 picks.1.pick_ref
  76.7 0.0 collective-permute-done.far_ref
  76.8 1.1 %broadcast_select_fusion = bf16[2,1024,128]{2,1,0:T(8,128)(2,1)S(1)} fusion(bf16[2,1024,128]{2,1,0:T(8,128)(2,1)} %collective-permute-done.far_ref, bf16[2,1024,128]{2,1,0:T(8,128)(2,1)} %pad_maximum_fusion, pred[]{:T(512)S(6)} %eq.5), kind=kLoop, calls=%fused_computation.1 | loop fusion | flops 262144 | bytes 1572865 | tf_op jit(solution)/shard_map/jit(_where)/select_n | solution.py:384
  77.9 0.3 collective-permute-start.1
  78.2 1.7 %collective-permute-done.1.near_ref = bf16[2,1024,128]{2,1,0:T(8,128)(2,1)S(1)} collective-permute-done((bf16[2,1024,128]{2,1,0:T(8,128)(2,1)S(1)}, bf16[2,1024,128]{2,1,0:T(8,128)(2,1)S(1)}, u32[]{:S(2)}, u32[]{:S(2)}) %collective-permute-start.1) | collective-permute-done | bytes 524320 | tf_op jit(solution)/shard_map/ppermute | solution.py:385
  79.9 0.0 copy-start.1
  79.9 0.9 copy-done.1
  80.8 0.0 copy-start.3
  80.8 0.9 copy-done.3
  81.8 5.3 %window_attention.1 = bf16[1024,128]{1,0:T(8,128)(2,1)} custom-call(s32[1]{0:T(128)} %bitcast.4.at_ref, bf16[1024,128]{1,0:T(8,128)(2,1)S(1)} %bitcast.13, bf16[1024,128]{1,0:T(8,128)(2,1)S(1)} %bitcast.10, bf16[1024,128]{1,0:T(8,128)(2,1)S(1)} %bitcast.11, bf16[2,1024,128]{2,1,0:T(8,128)(2,1)} %collective-permute-done.far_ref, ...), custom_call_target="tpu_custom_call" | custom-call | flops 1207959552 | bytes 2097152 | tf_op jit(solution)/shard_map/window_attention/pallas_call | solution.py:309
  87.1 6.0 %all-to-all-done.1.back_ref = bf16[32,128,128]{2,1,0:T(8,128)(2,1)S(1)} async-done(((bf16[32,128,128]{2,1,0:T(8,128)(2,1)}), bf16[32,128,128]{2,1,0:T(8,128)(2,1)S(1)}, u32[]{:S(2)}, u32[]{:S(2)}) %all-to-all-start.1) | async-done | bytes 1048608 | tf_op jit(solution)/shard_map/all_to_all | solution.py:383
  93.1 2.1 %unpack_slots.1 = bf16[1024,128]{1,0:T(8,128)(2,1)} custom-call(s32[8,128]{1,0:T(8,128)S(1)} %get-tuple-element.13.start_ref, bf16[1024,1024]{1,0:T(8,128)(2,1)S(1)} %picks.1.pick_ref, bf16[32,128,128]{2,1,0:T(8,128)(2,1)S(1)} %all-to-all-done.1.back_ref), custom_call_target="tpu_custom_call" | custom-call | tf_op jit(solution)/shard_map/unpack_slots/pallas_call | solution.py:355
Async XLA Ops:
  0.6 0.7 copy-start.2
  5.5 8.8 %copy-start = (bf16[1,1024,128]{2,1,0:T(8,128)(2,1)S(1)}, bf16[1,1024,128]{2,1,0:T(8,128)(2,1)}, u32[]{:S(2)}) copy-start(bf16[1,1024,128]{2,1,0:T(8,128)(2,1)} %param.12) | copy-start | bytes 786436
  5.5 48.5 %all-to-all-start = ((bf16[32,384,128]{2,1,0:T(8,128)(2,1)}), bf16[32,384,128]{2,1,0:T(8,128)(2,1)S(1)}, u32[]{:S(2)}, u32[]{:S(2)}) async-start(bf16[32,384,128]{2,1,0:T(8,128)(2,1)} %get-tuple-element.14), calls=%async_computation | async-start | bytes 6291456 | tf_op jit(solution)/shard_map/all_to_all | solution.py:375
  54.0 22.7 %collective-permute-start = (bf16[2,1024,128]{2,1,0:T(8,128)(2,1)}, bf16[2,1024,128]{2,1,0:T(8,128)(2,1)}, u32[]{:S(2)}, u32[]{:S(2)}) collective-permute-start(bf16[2,1024,128]{2,1,0:T(8,128)(2,1)} %pad_maximum_fusion), channel_id=1, source_target_pairs={{0,2},{1,3},{2,4},{3,5},{4,6},{5,7},{6,8},{7,9},{8,10},{9,11},{10,... | collective-permute-start | bytes 1572872 | tf_op jit(solution)/shard_map/ppermute | solution.py:368
  70.4 22.7 %all-to-all-start.1 = ((bf16[32,128,128]{2,1,0:T(8,128)(2,1)}), bf16[32,128,128]{2,1,0:T(8,128)(2,1)S(1)}, u32[]{:S(2)}, u32[]{:S(2)}) async-start(bf16[32,128,128]{2,1,0:T(8,128)(2,1)} %cluster_attention.1), calls=%async_computation.1 | async-start | bytes 2097152 | tf_op jit(solution)/shard_map/all_to_all | solution.py:383
  77.9 2.0 %collective-permute-start.1 = (bf16[2,1024,128]{2,1,0:T(8,128)(2,1)S(1)}, bf16[2,1024,128]{2,1,0:T(8,128)(2,1)S(1)}, u32[]{:S(2)}, u32[]{:S(2)}) collective-permute-start(bf16[2,1024,128]{2,1,0:T(8,128)(2,1)S(1)} %broadcast_select_fusion), channel_id=1, source_target_pairs={{0,1},{1,0},{2,3},{3,2},{4,5},{5,4},{6,7},{7,6},{8,9},{9,8},{10,11... | collective-permute-start | bytes 1572872 | tf_op jit(solution)/shard_map/ppermute | solution.py:385
  79.9 1.0 copy-start.1
  80.8 0.9 copy-start.3

commit v6 on v5

--- a/solution.py
+++ b/solution.py
@@ -16,8 +16,9 @@
 NEVER = -1e30
 EMPTY = 256.0
 GROUP = 8
-CHUNK = 1024
-SENDS = (0, 24, 32)
+CHUNK = 2048
+TILE = 256
+SENDS = {11: (8, 24), 15: (24, 32), 0: (0, 8)}
 VMEM = pl.BlockSpec(memory_space=pltpu.VMEM)
 HBM = pl.BlockSpec(memory_space=pltpu.HBM)
 
@@ -152,17 +153,24 @@
 
 def attend(tasks, query_of, key_ref, value_ref, write):
     def score(task):
-        block, low, high, mask, _, _ = task
+        block, low, high, head, tail, _, _ = task
         s = lax.dot_general(
             query_of(block),
             key_ref[low:high],
             (((1,), (1,)), ((), ())),
             preferred_element_type=jnp.float32,
         )
-        return s if mask is None else jnp.where(mask, s, NEVER)
+        if head is not None:
+            edge = head.shape[1]
+            s = jnp.concatenate([jnp.where(head, s[:, :edge], NEVER), s[:, edge:]], axis=1)
+        if tail is not None:
+            edge = high - low - tail.shape[1]
+            masked = jnp.where(tail, s[:, edge:], NEVER)
+            s = masked if edge == 0 else jnp.concatenate([s[:, :edge], masked], axis=1)
+        return s
 
     coming = score(tasks[0])
-    for t, (block, low, high, _, first, last) in enumerate(tasks):
+    for t, (block, low, high, _, _, first, last) in enumerate(tasks):
         s = coming
         if t + 1 < len(tasks):
             coming = score(tasks[t + 1])
@@ -181,10 +189,21 @@
             )
 
 
-def tasks_of(block, spans):
+def tasks_of(block, low, high, head, tail):
+    parts = -(-(high - low) // CHUNK)
+    steps = (high - low) // TILE
+    edges = [low + TILE * (steps * p // parts) for p in range(parts + 1)]
     return [
-        (block, low, high, mask, t == 0, t == len(spans) - 1)
-        for t, (low, high, mask) in enumerate(spans)
+        (
+            block,
+            edges[p],
+            edges[p + 1],
+            head if p == 0 else None,
+            tail if p == parts - 1 else None,
+            p == 0,
+            p == parts - 1,
+        )
+        for p in range(parts)
     ]
 
 
@@ -206,31 +225,32 @@
     within = lax.broadcasted_iota(jnp.int32, (size, size), 1) <= lax.broadcasted_iota(
         jnp.int32, (size, size), 0
     )
-    for s in range(blocks):
-        at = slice(s * CAP, (s + 1) * CAP)
-        key = got_ref[s, CAP : 2 * CAP].astype(jnp.float32)
-        used = key < 100.0
-        key_ref[at] = jnp.where(used, key, filler).astype(jnp.bfloat16)
-        value_ref[at, 0:D] = got_ref[s, 2 * CAP : 3 * CAP]
-        value_ref[at, D : 2 * D] = used.astype(jnp.float32).astype(jnp.bfloat16)
+    ready = set()
 
     def query_of(i):
+        for s in sorted(set(range(2 * i + 2)) - ready):
+            at = slice(s * CAP, (s + 1) * CAP)
+            key = got_ref[s, CAP : 2 * CAP].astype(jnp.float32)
+            used = key < 100.0
+            key_ref[at] = jnp.where(used, key, filler).astype(jnp.bfloat16)
+            value_ref[at, 0:D] = got_ref[s, 2 * CAP : 3 * CAP]
+            value_ref[at, D : 2 * D] = used.astype(jnp.float32).astype(jnp.bfloat16)
+            ready.add(s)
         return got_ref[2 * i : 2 * i + 2, 0:CAP].reshape(size, D)
 
     tasks = []
-    for i in range(blocks // 2):
-        own = i * size
-        spans = [(low, min(low + CHUNK, own), None) for low in range(0, own, CHUNK)]
-        tasks += tasks_of(i, spans + [(own, own + size, within)])
+    pairs = blocks // 2
+    for i in [*range(pairs // 4, pairs), *reversed(range(pairs // 4))]:
+        tasks += tasks_of(i, 0, (i + 1) * size, None, within)
     sends = []
 
     def write(i, mixed):
         mixed_ref[2 * i : 2 * i + 2] = mixed.reshape(2, CAP, D)
-        if 2 * i + 2 in SENDS:
-            n = SENDS.index(2 * i + 2)
-            part = pl.ds(SENDS[n - 1], SENDS[n] - SENDS[n - 1])
+        if i in SENDS:
+            n, (low, high) = list(SENDS).index(i), SENDS[i]
+            part = pl.ds(low, high - low)
             sends.append(
-                pltpu.make_async_copy(mixed_ref.at[part], out_ref.at[part], out_sems.at[n - 1])
+                pltpu.make_async_copy(mixed_ref.at[part], out_ref.at[part], out_sems.at[n])
             )
             sends[-1].start()
 
@@ -251,7 +271,7 @@
             pltpu.VMEM((slots, D), jnp.bfloat16),
             pltpu.VMEM((slots, 2 * D), jnp.bfloat16),
             pltpu.VMEM((blocks, CAP, D), jnp.bfloat16),
-            pltpu.SemaphoreType.DMA((len(SENDS) - 1,)),
+            pltpu.SemaphoreType.DMA((len(SENDS),)),
         ],
         compiler_params=params(),
         cost_estimate=pl.CostEstimate(
@@ -287,15 +307,7 @@
     tasks = []
     for i in range(TOK // size):
         low = i * size
-        high = low + 2 * TOK
-        middle = low + size + CHUNK
-        spans = [
-            (low, low + size, column > line),
-            (low + size, middle, None),
-            (middle, high, None),
-            (high, high + size, column <= line),
-        ]
-        tasks += tasks_of(i, spans)
+        tasks += tasks_of(i, low, low + 2 * TOK + size, column > line, column <= line)
 
     def write(i, mixed):
         out_ref[i * size : (i + 1) * size] = mixed

time: 95.8 us -> 94.9 us (level)
  transfers between devices with their start and end apart: 4 -> 4, of which waited for: 3 -> 3; matrix products, arithmetic and copies ran while one was open for 3% -> 3% of each run, Pallas kernels for 20% -> 19%
where the time goes in v6:
time: 94.9 us; the launch traced here: 94.4 us
  waiting for transfers between devices  45.7 us (48%)
  Pallas kernels  24.3 us (26%)
  starting transfers between devices  18.2 us (19%)
  other arithmetic  2.92 us (3%)
  local copies, waits for them, and re-layouts  2.59 us (3%)
    all_to_all x1, waiting for transfers between devices, local(): got = lax.all_to_all(sent, SEQ, split_axis=0, concat_axis=0, tiled=True)  37.9 us
    pallas_call x1, Pallas kernels, routed(): pl.pallas_call(routed_kernel, out_shape=pltpu.HBM((blocks, CAP, D), jnp.b...  12.1 us
    all_to_all x1, starting transfers between devices, local(): got = lax.all_to_all(sent, SEQ, split_axis=0, concat_axis=0, tiled=True)  8.73 us
    all_to_all x1, waiting for transfers between devices, local(): back = lax.all_to_all(mixed, SEQ, split_axis=0, concat_axis=0, tiled=True)  6.05 us
    all_to_all x1, starting transfers between devices, local(): back = lax.all_to_all(mixed, SEQ, split_axis=0, concat_axis=0, tiled=True)  5.81 us
    pallas_call x1, Pallas kernels, windowed(): pl.pallas_call(local_kernel, out_shape=jax.ShapeDtypeStruct((TOK, D), jnp...  5.3 us
    pallas_call x1, Pallas kernels, pack(): pl.pallas_call(pack_kernel, out_shape=(pltpu.HBM((CLUSTERS, 3 * CAP, D),...  4.2 us
    ppermute x1, starting transfers between devices, passed_along(): lax.ppermute(value, SEQ, [(s, s + steps) for s in range(count - steps)])  3.35 us
  transfers between devices with their start and end apart: 4, of which 3 were waited for; matrix products, arithmetic and copies ran while one was open for 3% of the time, Pallas kernels for 19%

profile of v6, /device:TPU:1, one launch (start us, length us, event | category | flops | bytes accessed | tf_op | source)
XLA Modules:
  0.0 94.4 jit_solution(11808216311320311544)
XLA Ops:
  0.6 0.0 copy-start.2
  0.6 0.7 copy-done.2
  1.3 4.2 %pack_slots.1 = (bf16[32,384,128]{2,1,0:T(8,128)(2,1)}, f32[8,1024]{1,0:T(8,128)S(1)}, s32[8,128]{1,0:T(8,128)S(1)}) custom-call(s32[1,1024]{1,0:T(1,128)S(1)} %bitcast.12, bf16[1024,128]{1,0:T(8,128)(2,1)} %bitcast.14, bf16[1024,128]{1,0:T(8,128)(2,1)} %bitcast.15, bf16[1024,128]{1,0:T(8,128)(2,1)} %bitcast.16), custom_call_target="tpu_custom_call" | custom-call | tf_op jit(solution)/shard_map/pack_slots/pallas_call | solution.py:131
  5.5 0.0 copy-start
  5.5 8.7 %all-to-all-start = ((bf16[32,384,128]{2,1,0:T(8,128)(2,1)}), bf16[32,384,128]{2,1,0:T(8,128)(2,1)S(1)}, u32[]{:S(2)}, u32[]{:S(2)}) async-start(bf16[32,384,128]{2,1,0:T(8,128)(2,1)} %get-tuple-element.14), calls=%async_computation | async-start | bytes 6291456 | tf_op jit(solution)/shard_map/all_to_all | solution.py:387
  14.3 0.0 copy-done
  14.3 1.8 %pad_maximum_fusion = bf16[2,1024,128]{2,1,0:T(8,128)(2,1)} fusion(bf16[1,1024,128]{2,1,0:T(8,128)(2,1)} %param.13, bf16[1,1024,128]{2,1,0:T(8,128)(2,1)S(1)} %copy-done), kind=kLoop, calls=%fused_computation | loop fusion | flops 262144 | bytes 1048576 | tf_op jit(solution)/shard_map/concatenate | solution.py:388
  16.1 37.9 %all-to-all-done.got_ref = bf16[32,384,128]{2,1,0:T(8,128)(2,1)S(1)} async-done(((bf16[32,384,128]{2,1,0:T(8,128)(2,1)}), bf16[32,384,128]{2,1,0:T(8,128)(2,1)S(1)}, u32[]{:S(2)}, u32[]{:S(2)}) %all-to-all-start) | async-done | bytes 3145760 | tf_op jit(solution)/shard_map/all_to_all | solution.py:387
  54.0 3.4 %collective-permute-start = (bf16[2,1024,128]{2,1,0:T(8,128)(2,1)}, bf16[2,1024,128]{2,1,0:T(8,128)(2,1)}, u32[]{:S(2)}, u32[]{:S(2)}) collective-permute-start(bf16[2,1024,128]{2,1,0:T(8,128)(2,1)} %pad_maximum_fusion), channel_id=1, source_target_pairs={{0,2},{1,3},{2,4},{3,5},{4,6},{5,7},{6,8},{7,9},{8,10},{9,11},{10,... | collective-permute-start | bytes 1572872 | tf_op jit(solution)/shard_map/ppermute | solution.py:380
  57.4 12.1 %cluster_attention.1 = bf16[32,128,128]{2,1,0:T(8,128)(2,1)} custom-call(bf16[32,384,128]{2,1,0:T(8,128)(2,1)S(1)} %all-to-all-done.got_ref), custom_call_target="tpu_custom_call" | custom-call | flops 8589934592 | bytes 4194304 | tf_op jit(solution)/shard_map/cluster_attention/pallas_call | solution.py:265
  69.5 5.8 %all-to-all-start.1 = ((bf16[32,128,128]{2,1,0:T(8,128)(2,1)}), bf16[32,128,128]{2,1,0:T(8,128)(2,1)S(1)}, u32[]{:S(2)}, u32[]{:S(2)}) async-start(bf16[32,128,128]{2,1,0:T(8,128)(2,1)} %cluster_attention.1), calls=%async_computation.1 | async-start | bytes 2097152 | tf_op jit(solution)/shard_map/all_to_all | solution.py:395
  75.4 0.5 picks.1.pick_ref
  75.9 0.0 collective-permute-done.far_ref
  75.9 1.1 %broadcast_select_fusion = bf16[2,1024,128]{2,1,0:T(8,128)(2,1)S(1)} fusion(bf16[2,1024,128]{2,1,0:T(8,128)(2,1)} %collective-permute-done.far_ref, bf16[2,1024,128]{2,1,0:T(8,128)(2,1)} %pad_maximum_fusion, pred[]{:T(512)S(6)} %eq.5), kind=kLoop, calls=%fused_computation.1 | loop fusion | flops 262144 | bytes 1572865 | tf_op jit(solution)/shard_map/jit(_where)/select_n | solution.py:396
  77.0 0.3 collective-permute-start.1
  77.3 1.7 %collective-permute-done.1.near_ref = bf16[2,1024,128]{2,1,0:T(8,128)(2,1)S(1)} collective-permute-done((bf16[2,1024,128]{2,1,0:T(8,128)(2,1)S(1)}, bf16[2,1024,128]{2,1,0:T(8,128)(2,1)S(1)}, u32[]{:S(2)}, u32[]{:S(2)}) %collective-permute-start.1) | collective-permute-done | bytes 524320 | tf_op jit(solution)/shard_map/ppermute | solution.py:397
  79.0 0.0 copy-start.1
  79.0 0.9 %copy-done.1 = bf16[1,1024,128]{2,1,0:T(8,128)(2,1)S(1)} copy-done((bf16[1,1024,128]{2,1,0:T(8,128)(2,1)S(1)}, bf16[1,1024,128]{2,1,0:T(8,128)(2,1)}, u32[]{:S(2)}) %copy-start.1) | copy-done | bytes 262168
  79.9 0.0 copy-start.3
  79.9 0.9 %copy-done.3 = bf16[1,1024,128]{2,1,0:T(8,128)(2,1)S(1)} copy-done((bf16[1,1024,128]{2,1,0:T(8,128)(2,1)S(1)}, bf16[1,1024,128]{2,1,0:T(8,128)(2,1)}, u32[]{:S(2)}) %copy-start.3) | copy-done | bytes 262168
  80.9 5.3 %window_attention.1 = bf16[1024,128]{1,0:T(8,128)(2,1)} custom-call(s32[1]{0:T(128)} %bitcast.4.at_ref, bf16[1024,128]{1,0:T(8,128)(2,1)S(1)} %bitcast.13, bf16[1024,128]{1,0:T(8,128)(2,1)S(1)} %bitcast.10, bf16[1024,128]{1,0:T(8,128)(2,1)S(1)} %bitcast.11, bf16[2,1024,128]{2,1,0:T(8,128)(2,1)} %collective-permute-done.far_ref, ...), custom_call_target="tpu_custom_call" | custom-call | flops 1207959552 | bytes 2097152 | tf_op jit(solution)/shard_map/window_attention/pallas_call | solution.py:321
  86.2 6.1 %all-to-all-done.1.back_ref = bf16[32,128,128]{2,1,0:T(8,128)(2,1)S(1)} async-done(((bf16[32,128,128]{2,1,0:T(8,128)(2,1)}), bf16[32,128,128]{2,1,0:T(8,128)(2,1)S(1)}, u32[]{:S(2)}, u32[]{:S(2)}) %all-to-all-start.1) | async-done | bytes 1048608 | tf_op jit(solution)/shard_map/all_to_all | solution.py:395
  92.2 2.2 %unpack_slots.1 = bf16[1024,128]{1,0:T(8,128)(2,1)} custom-call(s32[8,128]{1,0:T(8,128)S(1)} %get-tuple-element.13.start_ref, bf16[1024,1024]{1,0:T(8,128)(2,1)S(1)} %picks.1.pick_ref, bf16[32,128,128]{2,1,0:T(8,128)(2,1)S(1)} %all-to-all-done.1.back_ref), custom_call_target="tpu_custom_call" | custom-call | tf_op jit(solution)/shard_map/unpack_slots/pallas_call | solution.py:367
Async XLA Ops:
  0.6 0.7 copy-start.2
  5.5 8.8 %copy-start = (bf16[1,1024,128]{2,1,0:T(8,128)(2,1)S(1)}, bf16[1,1024,128]{2,1,0:T(8,128)(2,1)}, u32[]{:S(2)}) copy-start(bf16[1,1024,128]{2,1,0:T(8,128)(2,1)} %param.12) | copy-start | bytes 786436
  5.5 48.5 %all-to-all-start = ((bf16[32,384,128]{2,1,0:T(8,128)(2,1)}), bf16[32,384,128]{2,1,0:T(8,128)(2,1)S(1)}, u32[]{:S(2)}, u32[]{:S(2)}) async-start(bf16[32,384,128]{2,1,0:T(8,128)(2,1)} %get-tuple-element.14), calls=%async_computation | async-start | bytes 6291456 | tf_op jit(solution)/shard_map/all_to_all | solution.py:387
  54.0 21.8 %collective-permute-start = (bf16[2,1024,128]{2,1,0:T(8,128)(2,1)}, bf16[2,1024,128]{2,1,0:T(8,128)(2,1)}, u32[]{:S(2)}, u32[]{:S(2)}) collective-permute-start(bf16[2,1024,128]{2,1,0:T(8,128)(2,1)} %pad_maximum_fusion), channel_id=1, source_target_pairs={{0,2},{1,3},{2,4},{3,5},{4,6},{5,7},{6,8},{7,9},{8,10},{9,11},{10,... | collective-permute-start | bytes 1572872 | tf_op jit(solution)/shard_map/ppermute | solution.py:380
  69.5 22.7 %all-to-all-start.1 = ((bf16[32,128,128]{2,1,0:T(8,128)(2,1)}), bf16[32,128,128]{2,1,0:T(8,128)(2,1)S(1)}, u32[]{:S(2)}, u32[]{:S(2)}) async-start(bf16[32,128,128]{2,1,0:T(8,128)(2,1)} %cluster_attention.1), calls=%async_computation.1 | async-start | bytes 2097152 | tf_op jit(solution)/shard_map/all_to_all | solution.py:395
  77.0 2.0 %collective-permute-start.1 = (bf16[2,1024,128]{2,1,0:T(8,128)(2,1)S(1)}, bf16[2,1024,128]{2,1,0:T(8,128)(2,1)S(1)}, u32[]{:S(2)}, u32[]{:S(2)}) collective-permute-start(bf16[2,1024,128]{2,1,0:T(8,128)(2,1)S(1)} %broadcast_select_fusion), channel_id=1, source_target_pairs={{0,1},{1,0},{2,3},{3,2},{4,5},{5,4},{6,7},{7,6},{8,9},{9,8},{10,11... | collective-permute-start | bytes 1572872 | tf_op jit(solution)/shard_map/ppermute | solution.py:397
  79.0 1.0 %copy-start.1 = (bf16[1,1024,128]{2,1,0:T(8,128)(2,1)S(1)}, bf16[1,1024,128]{2,1,0:T(8,128)(2,1)}, u32[]{:S(2)}) copy-start(bf16[1,1024,128]{2,1,0:T(8,128)(2,1)} %param.13) | copy-start | bytes 786436
  79.9 0.9 %copy-start.3 = (bf16[1,1024,128]{2,1,0:T(8,128)(2,1)S(1)}, bf16[1,1024,128]{2,1,0:T(8,128)(2,1)}, u32[]{:S(2)}) copy-start(bf16[1,1024,128]{2,1,0:T(8,128)(2,1)} %param.11) | copy-start | bytes 786436

commit v7 on v6

--- a/solution.py
+++ b/solution.py
@@ -294,7 +294,7 @@
         filler = jnp.broadcast_to(start, (TOK, D))
         rows = pl.ds(b * TOK, TOK)
         key_ref[rows] = jnp.where(there, key.astype(jnp.float32), filler).astype(jnp.bfloat16)
-        value_ref[rows, 0:D] = value
+        value_ref[rows, 0:D] = jnp.where(there, value.astype(jnp.float32), 0.0).astype(jnp.bfloat16)
         value_ref[rows, D : 2 * D] = jnp.full((TOK, D), jnp.where(there, 1.0, 0.0)).astype(
             jnp.bfloat16
         )
@@ -377,7 +377,7 @@
 
 def passed_along(value, steps):
     count = lax.axis_size(SEQ)
-    return lax.ppermute(value, SEQ, [(s, s + steps) for s in range(count - steps)])
+    return lax.ppermute(value, SEQ, [(s, (s + steps) % count) for s in range(count)])
 
 
 def local(q_routed, k_routed, v_routed, memberships, q_local, k_local, v_local):

time: 94.9 us -> 92.9 us (0.979)
  starting transfers between devices: 18.2 us -> 16.3 us
    ppermute x1, starting transfers between devices: 3.35 us -> 0.61 us  [passed_along(): lax.ppermute(value, SEQ, [(s, (s + steps) % count) for s in range(count)])]
where the time goes in v7:
time: 92.9 us; the launch traced here: 92.4 us
  waiting for transfers between devices  45.7 us (49%)
  Pallas kernels  24.2 us (26%)
  starting transfers between devices  16.3 us (18%)
  other arithmetic  2.92 us (3%)
  local copies, waits for them, and re-layouts  2.59 us (3%)
    all_to_all x1, waiting for transfers between devices, local(): got = lax.all_to_all(sent, SEQ, split_axis=0, concat_axis=0, tiled=True)  37.9 us
    pallas_call x1, Pallas kernels, routed(): pl.pallas_call(routed_kernel, out_shape=pltpu.HBM((blocks, CAP, D), jnp.b...  12.1 us
    all_to_all x1, starting transfers between devices, local(): got = lax.all_to_all(sent, SEQ, split_axis=0, concat_axis=0, tiled=True)  8.73 us
    all_to_all x1, starting transfers between devices, local(): back = lax.all_to_all(mixed, SEQ, split_axis=0, concat_axis=0, tiled=True)  6.6 us
    all_to_all x1, waiting for transfers between devices, local(): back = lax.all_to_all(mixed, SEQ, split_axis=0, concat_axis=0, tiled=True)  6.09 us
    pallas_call x1, Pallas kernels, windowed(): pl.pallas_call(local_kernel, out_shape=jax.ShapeDtypeStruct((TOK, D), jnp...  5.26 us
    pallas_call x1, Pallas kernels, pack(): pl.pallas_call(pack_kernel, out_shape=(pltpu.HBM((CLUSTERS, 3 * CAP, D),...  4.2 us
    unnamed x8, local copies, waits for them, and re-layouts  2.59 us
  transfers between devices with their start and end apart: 4, of which 3 were waited for; matrix products, arithmetic and copies ran while one was open for 3% of the time, Pallas kernels for 19%

profile of v7, /device:TPU:1, one launch (start us, length us, event | category | flops | bytes accessed | tf_op | source)
XLA Modules:
  0.0 92.4 jit_solution(14808566929906222988)
XLA Ops:
  0.6 0.0 copy-start.2
  0.6 0.7 copy-done.2
  1.3 4.2 %pack_slots.1 = (bf16[32,384,128]{2,1,0:T(8,128)(2,1)}, f32[8,1024]{1,0:T(8,128)S(1)}, s32[8,128]{1,0:T(8,128)S(1)}) custom-call(s32[1,1024]{1,0:T(1,128)S(1)} %bitcast.12, bf16[1024,128]{1,0:T(8,128)(2,1)} %bitcast.14, bf16[1024,128]{1,0:T(8,128)(2,1)} %bitcast.15, bf16[1024,128]{1,0:T(8,128)(2,1)} %bitcast.16), custom_call_target="tpu_custom_call" | custom-call | tf_op jit(solution)/shard_map/pack_slots/pallas_call | solution.py:131
  5.5 0.0 copy-start
  5.5 8.7 %all-to-all-start = ((bf16[32,384,128]{2,1,0:T(8,128)(2,1)}), bf16[32,384,128]{2,1,0:T(8,128)(2,1)S(1)}, u32[]{:S(2)}, u32[]{:S(2)}) async-start(bf16[32,384,128]{2,1,0:T(8,128)(2,1)} %get-tuple-element.14), calls=%async_computation | async-start | bytes 6291456 | tf_op jit(solution)/shard_map/all_to_all | solution.py:387
  14.3 0.0 copy-done
  14.3 1.8 %pad_maximum_fusion = bf16[2,1024,128]{2,1,0:T(8,128)(2,1)} fusion(bf16[1,1024,128]{2,1,0:T(8,128)(2,1)} %param.13, bf16[1,1024,128]{2,1,0:T(8,128)(2,1)S(1)} %copy-done), kind=kLoop, calls=%fused_computation | loop fusion | flops 262144 | bytes 1048576 | tf_op jit(solution)/shard_map/concatenate | solution.py:388
  16.1 37.9 %all-to-all-done.got_ref = bf16[32,384,128]{2,1,0:T(8,128)(2,1)S(1)} async-done(((bf16[32,384,128]{2,1,0:T(8,128)(2,1)}), bf16[32,384,128]{2,1,0:T(8,128)(2,1)S(1)}, u32[]{:S(2)}, u32[]{:S(2)}) %all-to-all-start) | async-done | bytes 3145760 | tf_op jit(solution)/shard_map/all_to_all | solution.py:387
  54.0 0.6 collective-permute-start
  54.7 12.1 %cluster_attention.1 = bf16[32,128,128]{2,1,0:T(8,128)(2,1)} custom-call(bf16[32,384,128]{2,1,0:T(8,128)(2,1)S(1)} %all-to-all-done.got_ref), custom_call_target="tpu_custom_call" | custom-call | flops 8589934592 | bytes 4194304 | tf_op jit(solution)/shard_map/cluster_attention/pallas_call | solution.py:265
  66.8 6.6 %all-to-all-start.1 = ((bf16[32,128,128]{2,1,0:T(8,128)(2,1)}), bf16[32,128,128]{2,1,0:T(8,128)(2,1)S(1)}, u32[]{:S(2)}, u32[]{:S(2)}) async-start(bf16[32,128,128]{2,1,0:T(8,128)(2,1)} %cluster_attention.1), calls=%async_computation.1 | async-start | bytes 2097152 | tf_op jit(solution)/shard_map/all_to_all | solution.py:395
  73.4 0.5 picks.1.pick_ref
  73.9 0.0 collective-permute-done.far_ref
  73.9 1.1 %broadcast_select_fusion = bf16[2,1024,128]{2,1,0:T(8,128)(2,1)S(1)} fusion(bf16[2,1024,128]{2,1,0:T(8,128)(2,1)} %collective-permute-done.far_ref, bf16[2,1024,128]{2,1,0:T(8,128)(2,1)} %pad_maximum_fusion, pred[]{:T(512)S(6)} %eq.5), kind=kLoop, calls=%fused_computation.1 | loop fusion | flops 262144 | bytes 1572865 | tf_op jit(solution)/shard_map/jit(_where)/select_n | solution.py:396
  75.0 0.3 collective-permute-start.1
  75.4 1.7 %collective-permute-done.1.near_ref = bf16[2,1024,128]{2,1,0:T(8,128)(2,1)S(1)} collective-permute-done((bf16[2,1024,128]{2,1,0:T(8,128)(2,1)S(1)}, bf16[2,1024,128]{2,1,0:T(8,128)(2,1)S(1)}, u32[]{:S(2)}, u32[]{:S(2)}) %collective-permute-start.1) | collective-permute-done | bytes 524320 | tf_op jit(solution)/shard_map/ppermute | solution.py:397
  77.0 0.0 copy-start.1
  77.0 0.9 %copy-done.1 = bf16[1,1024,128]{2,1,0:T(8,128)(2,1)S(1)} copy-done((bf16[1,1024,128]{2,1,0:T(8,128)(2,1)S(1)}, bf16[1,1024,128]{2,1,0:T(8,128)(2,1)}, u32[]{:S(2)}) %copy-start.1) | copy-done | bytes 262168
  78.0 0.0 copy-start.3
  78.0 0.9 %copy-done.3 = bf16[1,1024,128]{2,1,0:T(8,128)(2,1)S(1)} copy-done((bf16[1,1024,128]{2,1,0:T(8,128)(2,1)S(1)}, bf16[1,1024,128]{2,1,0:T(8,128)(2,1)}, u32[]{:S(2)}) %copy-start.3) | copy-done | bytes 262168
  78.9 5.3 %window_attention.1 = bf16[1024,128]{1,0:T(8,128)(2,1)} custom-call(s32[1]{0:T(128)} %bitcast.4.at_ref, bf16[1024,128]{1,0:T(8,128)(2,1)S(1)} %bitcast.13, bf16[1024,128]{1,0:T(8,128)(2,1)S(1)} %bitcast.10, bf16[1024,128]{1,0:T(8,128)(2,1)S(1)} %bitcast.11, bf16[2,1024,128]{2,1,0:T(8,128)(2,1)} %collective-permute-done.far_ref, ...), custom_call_target="tpu_custom_call" | custom-call | flops 1207959552 | bytes 2097152 | tf_op jit(solution)/shard_map/window_attention/pallas_call | solution.py:321
  84.2 6.1 %all-to-all-done.1.back_ref = bf16[32,128,128]{2,1,0:T(8,128)(2,1)S(1)} async-done(((bf16[32,128,128]{2,1,0:T(8,128)(2,1)}), bf16[32,128,128]{2,1,0:T(8,128)(2,1)S(1)}, u32[]{:S(2)}, u32[]{:S(2)}) %all-to-all-start.1) | async-done | bytes 1048608 | tf_op jit(solution)/shard_map/all_to_all | solution.py:395
  90.3 2.1 %unpack_slots.1 = bf16[1024,128]{1,0:T(8,128)(2,1)} custom-call(s32[8,128]{1,0:T(8,128)S(1)} %get-tuple-element.13.start_ref, bf16[1024,1024]{1,0:T(8,128)(2,1)S(1)} %picks.1.pick_ref, bf16[32,128,128]{2,1,0:T(8,128)(2,1)S(1)} %all-to-all-done.1.back_ref), custom_call_target="tpu_custom_call" | custom-call | tf_op jit(solution)/shard_map/unpack_slots/pallas_call | solution.py:367
Async XLA Ops:
  0.6 0.7 copy-start.2
  5.5 8.8 %copy-start = (bf16[1,1024,128]{2,1,0:T(8,128)(2,1)S(1)}, bf16[1,1024,128]{2,1,0:T(8,128)(2,1)}, u32[]{:S(2)}) copy-start(bf16[1,1024,128]{2,1,0:T(8,128)(2,1)} %param.12) | copy-start | bytes 786436
  5.5 48.5 %all-to-all-start = ((bf16[32,384,128]{2,1,0:T(8,128)(2,1)}), bf16[32,384,128]{2,1,0:T(8,128)(2,1)S(1)}, u32[]{:S(2)}, u32[]{:S(2)}) async-start(bf16[32,384,128]{2,1,0:T(8,128)(2,1)} %get-tuple-element.14), calls=%async_computation | async-start | bytes 6291456 | tf_op jit(solution)/shard_map/all_to_all | solution.py:387
  54.0 19.9 %collective-permute-start = (bf16[2,1024,128]{2,1,0:T(8,128)(2,1)}, bf16[2,1024,128]{2,1,0:T(8,128)(2,1)}, u32[]{:S(2)}, u32[]{:S(2)}) collective-permute-start(bf16[2,1024,128]{2,1,0:T(8,128)(2,1)} %pad_maximum_fusion), channel_id=1, source_target_pairs={{0,2},{1,3},{2,4},{3,5},{4,6},{5,7},{6,8},{7,9},{8,10},{9,11},{10,... | collective-permute-start | bytes 1572872 | tf_op jit(solution)/shard_map/ppermute | solution.py:380
  66.8 23.5 %all-to-all-start.1 = ((bf16[32,128,128]{2,1,0:T(8,128)(2,1)}), bf16[32,128,128]{2,1,0:T(8,128)(2,1)S(1)}, u32[]{:S(2)}, u32[]{:S(2)}) async-start(bf16[32,128,128]{2,1,0:T(8,128)(2,1)} %cluster_attention.1), calls=%async_computation.1 | async-start | bytes 2097152 | tf_op jit(solution)/shard_map/all_to_all | solution.py:395
  75.0 2.0 %collective-permute-start.1 = (bf16[2,1024,128]{2,1,0:T(8,128)(2,1)S(1)}, bf16[2,1024,128]{2,1,0:T(8,128)(2,1)S(1)}, u32[]{:S(2)}, u32[]{:S(2)}) collective-permute-start(bf16[2,1024,128]{2,1,0:T(8,128)(2,1)S(1)} %broadcast_select_fusion), channel_id=1, source_target_pairs={{0,1},{1,0},{2,3},{3,2},{4,5},{5,4},{6,7},{7,6},{8,9},{9,8},{10,11... | collective-permute-start | bytes 1572872 | tf_op jit(solution)/shard_map/ppermute | solution.py:397
  77.0 1.0 %copy-start.1 = (bf16[1,1024,128]{2,1,0:T(8,128)(2,1)S(1)}, bf16[1,1024,128]{2,1,0:T(8,128)(2,1)}, u32[]{:S(2)}) copy-start(bf16[1,1024,128]{2,1,0:T(8,128)(2,1)} %param.13) | copy-start | bytes 786436
  78.0 0.9 %copy-start.3 = (bf16[1,1024,128]{2,1,0:T(8,128)(2,1)S(1)}, bf16[1,1024,128]{2,1,0:T(8,128)(2,1)}, u32[]{:S(2)}) copy-start(bf16[1,1024,128]{2,1,0:T(8,128)(2,1)} %param.11) | copy-start | bytes 786436

commit v8 on v7

--- a/solution.py
+++ b/solution.py
@@ -151,11 +151,19 @@
     )(ids, in_hbm(q), in_hbm(k), in_hbm(v))
 
 
+def put_keys(key_ref, rows, key):
+    scaled = key * EXP_SCALE
+    high = scaled.astype(jnp.bfloat16)
+    key_ref[rows, 0:D] = high
+    key_ref[rows, D : 2 * D] = (scaled - high.astype(jnp.float32)).astype(jnp.bfloat16)
+
+
 def attend(tasks, query_of, key_ref, value_ref, write):
     def score(task):
         block, low, high, head, tail, _, _ = task
+        queries = query_of(block)
         s = lax.dot_general(
-            query_of(block),
+            jnp.concatenate([queries, queries], axis=1),
             key_ref[low:high],
             (((1,), (1,)), ((), ())),
             preferred_element_type=jnp.float32,
@@ -177,10 +185,10 @@
         top = jnp.max(s, axis=1, keepdims=True)
         if not first:
             top = jnp.maximum(top, top_before)
-        weight = jnp.exp2(s * EXP_SCALE - top * EXP_SCALE).astype(jnp.bfloat16)
+        weight = jnp.exp2(s - top).astype(jnp.bfloat16)
         total = jnp.dot(weight, value_ref[low:high], preferred_element_type=jnp.float32)
         if not first:
-            total = total + total_before * jnp.exp2((top_before - top) * EXP_SCALE)
+            total = total + total_before * jnp.exp2(top_before - top)
         top_before, total_before = top, total
         if last:
             mass = total[:, D : 2 * D]
@@ -232,7 +240,7 @@
             at = slice(s * CAP, (s + 1) * CAP)
             key = got_ref[s, CAP : 2 * CAP].astype(jnp.float32)
             used = key < 100.0
-            key_ref[at] = jnp.where(used, key, filler).astype(jnp.bfloat16)
+            put_keys(key_ref, at, jnp.where(used, key, filler))
             value_ref[at, 0:D] = got_ref[s, 2 * CAP : 3 * CAP]
             value_ref[at, D : 2 * D] = used.astype(jnp.float32).astype(jnp.bfloat16)
             ready.add(s)
@@ -268,7 +276,7 @@
         in_specs=[VMEM],
         out_specs=HBM,
         scratch_shapes=[
-            pltpu.VMEM((slots, D), jnp.bfloat16),
+            pltpu.VMEM((slots, 2 * D), jnp.bfloat16),
             pltpu.VMEM((slots, 2 * D), jnp.bfloat16),
             pltpu.VMEM((blocks, CAP, D), jnp.bfloat16),
             pltpu.SemaphoreType.DMA((len(SENDS),)),
@@ -293,12 +301,12 @@
         start = jnp.where(at == 0, own, nearest)
         filler = jnp.broadcast_to(start, (TOK, D))
         rows = pl.ds(b * TOK, TOK)
-        key_ref[rows] = jnp.where(there, key.astype(jnp.float32), filler).astype(jnp.bfloat16)
+        put_keys(key_ref, rows, jnp.where(there, key.astype(jnp.float32), filler))
         value_ref[rows, 0:D] = jnp.where(there, value.astype(jnp.float32), 0.0).astype(jnp.bfloat16)
         value_ref[rows, D : 2 * D] = jnp.full((TOK, D), jnp.where(there, 1.0, 0.0)).astype(
             jnp.bfloat16
         )
-    key_ref[2 * TOK : 3 * TOK] = k_ref[...]
+    put_keys(key_ref, slice(2 * TOK, 3 * TOK), k_ref[...].astype(jnp.float32))
     value_ref[2 * TOK : 3 * TOK, 0:D] = v_ref[...]
     value_ref[2 * TOK : 3 * TOK, D : 2 * D] = jnp.ones((TOK, D), jnp.bfloat16)
     size = 256
@@ -324,7 +332,7 @@
         in_specs=[pl.BlockSpec(memory_space=pltpu.SMEM)] + [VMEM] * 5,
         out_specs=VMEM,
         scratch_shapes=[
-            pltpu.VMEM((3 * TOK, D), jnp.bfloat16),
+            pltpu.VMEM((3 * TOK, 2 * D), jnp.bfloat16),
             pltpu.VMEM((3 * TOK, 2 * D), jnp.bfloat16),
         ],
         compiler_params=params(),

time: 92.9 us -> 92.1 us (level)
  no operation moved by 1% of the time
where the time goes in v8:
time: 92.1 us; the launch traced here: 91.6 us
  waiting for transfers between devices  45.6 us (50%)
  Pallas kernels  23.3 us (25%)
  starting transfers between devices  16.5 us (18%)
  other arithmetic  2.92 us (3%)
  local copies, waits for them, and re-layouts  2.59 us (3%)
    all_to_all x1, waiting for transfers between devices, local(): got = lax.all_to_all(sent, SEQ, split_axis=0, concat_axis=0, tiled=True)  37.9 us
    pallas_call x1, Pallas kernels, routed(): pl.pallas_call(routed_kernel, out_shape=pltpu.HBM((blocks, CAP, D), jnp.b...  11.3 us
    all_to_all x1, starting transfers between devices, local(): got = lax.all_to_all(sent, SEQ, split_axis=0, concat_axis=0, tiled=True)  8.73 us
    all_to_all x1, starting transfers between devices, local(): back = lax.all_to_all(mixed, SEQ, split_axis=0, concat_axis=0, tiled=True)  6.6 us
    all_to_all x1, waiting for transfers between devices, local(): back = lax.all_to_all(mixed, SEQ, split_axis=0, concat_axis=0, tiled=True)  5.98 us
    pallas_call x1, Pallas kernels, windowed(): pl.pallas_call(local_kernel, out_shape=jax.ShapeDtypeStruct((TOK, D), jnp...  5.15 us
    pallas_call x1, Pallas kernels, pack(): pl.pallas_call(pack_kernel, out_shape=(pltpu.HBM((CLUSTERS, 3 * CAP, D),...  4.2 us
    unnamed x8, local copies, waits for them, and re-layouts  2.59 us
  transfers between devices with their start and end apart: 4, of which 3 were waited for; matrix products, arithmetic and copies ran while one was open for 3% of the time, Pallas kernels for 19%

profile of v8, /device:TPU:1, one launch (start us, length us, event | category | flops | bytes accessed | tf_op | source)
XLA Modules:
  0.0 91.6 jit_solution(13990206608632938133)
XLA Ops:
  0.6 0.0 copy-start.2
  0.6 0.7 copy-done.2
  1.3 4.2 %pack_slots.1 = (bf16[32,384,128]{2,1,0:T(8,128)(2,1)}, f32[8,1024]{1,0:T(8,128)S(1)}, s32[8,128]{1,0:T(8,128)S(1)}) custom-call(s32[1,1024]{1,0:T(1,128)S(1)} %bitcast.12, bf16[1024,128]{1,0:T(8,128)(2,1)} %bitcast.14, bf16[1024,128]{1,0:T(8,128)(2,1)} %bitcast.15, bf16[1024,128]{1,0:T(8,128)(2,1)} %bitcast.16), custom_call_target="tpu_custom_call" | custom-call | tf_op jit(solution)/shard_map/pack_slots/pallas_call | solution.py:131
  5.5 0.0 copy-start
  5.5 8.7 %all-to-all-start = ((bf16[32,384,128]{2,1,0:T(8,128)(2,1)}), bf16[32,384,128]{2,1,0:T(8,128)(2,1)S(1)}, u32[]{:S(2)}, u32[]{:S(2)}) async-start(bf16[32,384,128]{2,1,0:T(8,128)(2,1)} %get-tuple-element.14), calls=%async_computation | async-start | bytes 6291456 | tf_op jit(solution)/shard_map/all_to_all | solution.py:395
  14.3 0.0 copy-done
  14.3 1.8 %pad_maximum_fusion = bf16[2,1024,128]{2,1,0:T(8,128)(2,1)} fusion(bf16[1,1024,128]{2,1,0:T(8,128)(2,1)} %param.13, bf16[1,1024,128]{2,1,0:T(8,128)(2,1)S(1)} %copy-done), kind=kLoop, calls=%fused_computation | loop fusion | flops 262144 | bytes 1048576 | tf_op jit(solution)/shard_map/concatenate | solution.py:396
  16.1 37.9 %all-to-all-done.got_ref = bf16[32,384,128]{2,1,0:T(8,128)(2,1)S(1)} async-done(((bf16[32,384,128]{2,1,0:T(8,128)(2,1)}), bf16[32,384,128]{2,1,0:T(8,128)(2,1)S(1)}, u32[]{:S(2)}, u32[]{:S(2)}) %all-to-all-start) | async-done | bytes 3145760 | tf_op jit(solution)/shard_map/all_to_all | solution.py:395
  54.0 0.6 collective-permute-start
  54.7 11.3 %cluster_attention.1 = bf16[32,128,128]{2,1,0:T(8,128)(2,1)} custom-call(bf16[32,384,128]{2,1,0:T(8,128)(2,1)S(1)} %all-to-all-done.got_ref), custom_call_target="tpu_custom_call" | custom-call | flops 8589934592 | bytes 4194304 | tf_op jit(solution)/shard_map/cluster_attention/pallas_call | solution.py:273
  66.0 6.6 %all-to-all-start.1 = ((bf16[32,128,128]{2,1,0:T(8,128)(2,1)}), bf16[32,128,128]{2,1,0:T(8,128)(2,1)S(1)}, u32[]{:S(2)}, u32[]{:S(2)}) async-start(bf16[32,128,128]{2,1,0:T(8,128)(2,1)} %cluster_attention.1), calls=%async_computation.1 | async-start | bytes 2097152 | tf_op jit(solution)/shard_map/all_to_all | solution.py:403
  72.6 0.5 picks.1.pick_ref
  73.1 0.0 collective-permute-done.far_ref
  73.1 1.1 %broadcast_select_fusion = bf16[2,1024,128]{2,1,0:T(8,128)(2,1)S(1)} fusion(bf16[2,1024,128]{2,1,0:T(8,128)(2,1)} %collective-permute-done.far_ref, bf16[2,1024,128]{2,1,0:T(8,128)(2,1)} %pad_maximum_fusion, pred[]{:T(512)S(6)} %eq.5), kind=kLoop, calls=%fused_computation.1 | loop fusion | flops 262144 | bytes 1572865 | tf_op jit(solution)/shard_map/jit(_where)/select_n | solution.py:404
  74.2 0.5 collective-permute-start.1
  74.8 1.7 %collective-permute-done.1.near_ref = bf16[2,1024,128]{2,1,0:T(8,128)(2,1)S(1)} collective-permute-done((bf16[2,1024,128]{2,1,0:T(8,128)(2,1)S(1)}, bf16[2,1024,128]{2,1,0:T(8,128)(2,1)S(1)}, u32[]{:S(2)}, u32[]{:S(2)}) %collective-permute-start.1) | collective-permute-done | bytes 524320 | tf_op jit(solution)/shard_map/ppermute | solution.py:405
  76.5 0.0 copy-start.1
  76.5 0.9 %copy-done.1 = bf16[1,1024,128]{2,1,0:T(8,128)(2,1)S(1)} copy-done((bf16[1,1024,128]{2,1,0:T(8,128)(2,1)S(1)}, bf16[1,1024,128]{2,1,0:T(8,128)(2,1)}, u32[]{:S(2)}) %copy-start.1) | copy-done | bytes 262168
  77.4 0.0 copy-start.3
  77.4 0.9 %copy-done.3 = bf16[1,1024,128]{2,1,0:T(8,128)(2,1)S(1)} copy-done((bf16[1,1024,128]{2,1,0:T(8,128)(2,1)S(1)}, bf16[1,1024,128]{2,1,0:T(8,128)(2,1)}, u32[]{:S(2)}) %copy-start.3) | copy-done | bytes 262168
  78.4 5.2 %window_attention.1 = bf16[1024,128]{1,0:T(8,128)(2,1)} custom-call(s32[1]{0:T(128)} %bitcast.4.at_ref, bf16[1024,128]{1,0:T(8,128)(2,1)S(1)} %bitcast.13, bf16[1024,128]{1,0:T(8,128)(2,1)S(1)} %bitcast.10, bf16[1024,128]{1,0:T(8,128)(2,1)S(1)} %bitcast.11, bf16[2,1024,128]{2,1,0:T(8,128)(2,1)} %collective-permute-done.far_ref, ...), custom_call_target="tpu_custom_call" | custom-call | flops 1207959552 | bytes 2097152 | tf_op jit(solution)/shard_map/window_attention/pallas_call | solution.py:329
  83.5 6.0 %all-to-all-done.1.back_ref = bf16[32,128,128]{2,1,0:T(8,128)(2,1)S(1)} async-done(((bf16[32,128,128]{2,1,0:T(8,128)(2,1)}), bf16[32,128,128]{2,1,0:T(8,128)(2,1)S(1)}, u32[]{:S(2)}, u32[]{:S(2)}) %all-to-all-start.1) | async-done | bytes 1048608 | tf_op jit(solution)/shard_map/all_to_all | solution.py:403
  89.5 2.1 %unpack_slots.1 = bf16[1024,128]{1,0:T(8,128)(2,1)} custom-call(s32[8,128]{1,0:T(8,128)S(1)} %get-tuple-element.13.start_ref, bf16[1024,1024]{1,0:T(8,128)(2,1)S(1)} %picks.1.pick_ref, bf16[32,128,128]{2,1,0:T(8,128)(2,1)S(1)} %all-to-all-done.1.back_ref), custom_call_target="tpu_custom_call" | custom-call | tf_op jit(solution)/shard_map/unpack_slots/pallas_call | solution.py:375
Async XLA Ops:
  0.6 0.7 copy-start.2
  5.5 8.8 %copy-start = (bf16[1,1024,128]{2,1,0:T(8,128)(2,1)S(1)}, bf16[1,1024,128]{2,1,0:T(8,128)(2,1)}, u32[]{:S(2)}) copy-start(bf16[1,1024,128]{2,1,0:T(8,128)(2,1)} %param.12) | copy-start | bytes 786436
  5.5 48.5 %all-to-all-start = ((bf16[32,384,128]{2,1,0:T(8,128)(2,1)}), bf16[32,384,128]{2,1,0:T(8,128)(2,1)S(1)}, u32[]{:S(2)}, u32[]{:S(2)}) async-start(bf16[32,384,128]{2,1,0:T(8,128)(2,1)} %get-tuple-element.14), calls=%async_computation | async-start | bytes 6291456 | tf_op jit(solution)/shard_map/all_to_all | solution.py:395
  54.0 19.1 %collective-permute-start = (bf16[2,1024,128]{2,1,0:T(8,128)(2,1)}, bf16[2,1024,128]{2,1,0:T(8,128)(2,1)}, u32[]{:S(2)}, u32[]{:S(2)}) collective-permute-start(bf16[2,1024,128]{2,1,0:T(8,128)(2,1)} %pad_maximum_fusion), channel_id=1, source_target_pairs={{0,2},{1,3},{2,4},{3,5},{4,6},{5,7},{6,8},{7,9},{8,10},{9,11},{10,... | collective-permute-start | bytes 1572872 | tf_op jit(solution)/shard_map/ppermute | solution.py:388
  66.0 23.5 %all-to-all-start.1 = ((bf16[32,128,128]{2,1,0:T(8,128)(2,1)}), bf16[32,128,128]{2,1,0:T(8,128)(2,1)S(1)}, u32[]{:S(2)}, u32[]{:S(2)}) async-start(bf16[32,128,128]{2,1,0:T(8,128)(2,1)} %cluster_attention.1), calls=%async_computation.1 | async-start | bytes 2097152 | tf_op jit(solution)/shard_map/all_to_all | solution.py:403
  74.2 2.2 %collective-permute-start.1 = (bf16[2,1024,128]{2,1,0:T(8,128)(2,1)S(1)}, bf16[2,1024,128]{2,1,0:T(8,128)(2,1)S(1)}, u32[]{:S(2)}, u32[]{:S(2)}) collective-permute-start(bf16[2,1024,128]{2,1,0:T(8,128)(2,1)S(1)} %broadcast_select_fusion), channel_id=1, source_target_pairs={{0,1},{1,0},{2,3},{3,2},{4,5},{5,4},{6,7},{7,6},{8,9},{9,8},{10,11... | collective-permute-start | bytes 1572872 | tf_op jit(solution)/shard_map/ppermute | solution.py:405
  76.5 1.0 %copy-start.1 = (bf16[1,1024,128]{2,1,0:T(8,128)(2,1)S(1)}, bf16[1,1024,128]{2,1,0:T(8,128)(2,1)}, u32[]{:S(2)}) copy-start(bf16[1,1024,128]{2,1,0:T(8,128)(2,1)} %param.13) | copy-start | bytes 786436
  77.4 0.9 %copy-start.3 = (bf16[1,1024,128]{2,1,0:T(8,128)(2,1)S(1)}, bf16[1,1024,128]{2,1,0:T(8,128)(2,1)}, u32[]{:S(2)}) copy-start(bf16[1,1024,128]{2,1,0:T(8,128)(2,1)} %param.11) | copy-start | bytes 786436

commit v9 on v8

--- a/solution.py
+++ b/solution.py
@@ -43,6 +43,7 @@
     sent_ref,
     place_ref,
     start_ref,
+    ids_vmem,
     rows_ref,
     sorted_ref,
     stage_ref,
@@ -50,14 +51,18 @@
     in_sems,
     out_sems,
     start_sem,
+    ids_sem,
 ):
+    named = pltpu.make_async_copy(ids_ref, ids_vmem, ids_sem)
+    named.start()
     loads = [
         pltpu.make_async_copy(ref, rows_ref.at[i], in_sems.at[i])
         for i, ref in enumerate((q_ref, k_ref, v_ref))
     ]
     for load in loads:
         load.start()
-    ids = ids_ref[...]
+    named.wait()
+    ids = ids_vmem[...]
     cluster = lax.broadcasted_iota(jnp.int32, (CLUSTERS, TOK), 0)
     member = (ids == cluster).astype(jnp.float32)
     member_b = member.astype(jnp.bfloat16)
@@ -135,9 +140,10 @@
             pltpu.VMEM((8, TOK), jnp.float32),
             pltpu.VMEM((8, 128), jnp.int32),
         ),
-        in_specs=[VMEM] + [HBM] * 3,
+        in_specs=[HBM] * 4,
         out_specs=(HBM, VMEM, VMEM),
         scratch_shapes=[
+            pltpu.VMEM((1, TOK), jnp.int32),
             pltpu.VMEM((3, TOK, D), jnp.bfloat16),
             pltpu.VMEM((3, TOK + CAP, D), jnp.float32),
             pltpu.VMEM((CLUSTERS, 3 * CAP, D), jnp.bfloat16),
@@ -145,10 +151,11 @@
             pltpu.SemaphoreType.DMA((3,)),
             pltpu.SemaphoreType.DMA((CLUSTERS // GROUP,)),
             pltpu.SemaphoreType.DMA,
+            pltpu.SemaphoreType.DMA,
         ],
         compiler_params=params(),
         name="pack_slots",
-    )(ids, in_hbm(q), in_hbm(k), in_hbm(v))
+    )(in_hbm(ids), in_hbm(q), in_hbm(k), in_hbm(v))
 
 
 def put_keys(key_ref, rows, key):

time: 92.1 us -> 91.9 us (level)
    unnamed x8 -> x6, local copies, waits for them, and re-layouts: 2.59 us -> 1.91 us
where the time goes in v9:
time: 91.9 us; the launch traced here: 91.4 us
  waiting for transfers between devices  45.6 us (50%)
  Pallas kernels  23.8 us (26%)
  starting transfers between devices  16.5 us (18%)
  other arithmetic  2.9 us (3%)
  local copies, waits for them, and re-layouts  1.91 us (2%)
    all_to_all x1, waiting for transfers between devices, local(): got = lax.all_to_all(sent, SEQ, split_axis=0, concat_axis=0, tiled=True)  38 us
    pallas_call x1, Pallas kernels, routed(): pl.pallas_call(routed_kernel, out_shape=pltpu.HBM((blocks, CAP, D), jnp.b...  11.3 us
    all_to_all x1, starting transfers between devices, local(): got = lax.all_to_all(sent, SEQ, split_axis=0, concat_axis=0, tiled=True)  8.73 us
    all_to_all x1, starting transfers between devices, local(): back = lax.all_to_all(mixed, SEQ, split_axis=0, concat_axis=0, tiled=True)  6.6 us
    all_to_all x1, waiting for transfers between devices, local(): back = lax.all_to_all(mixed, SEQ, split_axis=0, concat_axis=0, tiled=True)  5.99 us
    pallas_call x1, Pallas kernels, windowed(): pl.pallas_call(local_kernel, out_shape=jax.ShapeDtypeStruct((TOK, D), jnp...  5.14 us
    pallas_call x1, Pallas kernels, pack(): pl.pallas_call(pack_kernel, out_shape=(pltpu.HBM((CLUSTERS, 3 * CAP, D),...  4.66 us
    pallas_call x1, Pallas kernels, unpack(): pl.pallas_call(unpack_kernel, out_shape=jax.ShapeDtypeStruct((TOK, D), jn...  2.15 us
  transfers between devices with their start and end apart: 4, of which 3 were waited for; matrix products, arithmetic and copies ran while one was open for 3% of the time, Pallas kernels for 19%

profile of v9, /device:TPU:1, one launch (start us, length us, event | category | flops | bytes accessed | tf_op | source)
XLA Modules:
  0.0 91.4 jit_solution(11028256344548154145)
XLA Ops:
  0.6 4.7 %pack_slots.1 = (bf16[32,384,128]{2,1,0:T(8,128)(2,1)}, f32[8,1024]{1,0:T(8,128)S(1)}, s32[8,128]{1,0:T(8,128)S(1)}) custom-call(s32[1,1024]{1,0:T(1,128)} %bitcast.17, bf16[1024,128]{1,0:T(8,128)(2,1)} %bitcast.13, bf16[1024,128]{1,0:T(8,128)(2,1)} %bitcast.14, bf16[1024,128]{1,0:T(8,128)(2,1)} %bitcast.15), custom_call_target="tpu_custom_call" | custom-call | tf_op jit(solution)/shard_map/pack_slots/pallas_call | solution.py:136
  5.3 0.0 copy-start
  5.3 8.7 %all-to-all-start = ((bf16[32,384,128]{2,1,0:T(8,128)(2,1)}), bf16[32,384,128]{2,1,0:T(8,128)(2,1)S(1)}, u32[]{:S(2)}, u32[]{:S(2)}) async-start(bf16[32,384,128]{2,1,0:T(8,128)(2,1)} %get-tuple-element.14), calls=%async_computation | async-start | bytes 6291456 | tf_op jit(solution)/shard_map/all_to_all | solution.py:402
  14.1 0.0 copy-done
  14.1 1.8 %pad_maximum_fusion = bf16[2,1024,128]{2,1,0:T(8,128)(2,1)} fusion(bf16[1,1024,128]{2,1,0:T(8,128)(2,1)} %param.13, bf16[1,1024,128]{2,1,0:T(8,128)(2,1)S(1)} %copy-done), kind=kLoop, calls=%fused_computation | loop fusion | flops 262144 | bytes 1048576 | tf_op jit(solution)/shard_map/concatenate | solution.py:403
  15.9 38.0 %all-to-all-done.got_ref = bf16[32,384,128]{2,1,0:T(8,128)(2,1)S(1)} async-done(((bf16[32,384,128]{2,1,0:T(8,128)(2,1)}), bf16[32,384,128]{2,1,0:T(8,128)(2,1)S(1)}, u32[]{:S(2)}, u32[]{:S(2)}) %all-to-all-start) | async-done | bytes 3145760 | tf_op jit(solution)/shard_map/all_to_all | solution.py:402
  53.8 0.6 collective-permute-start
  54.4 11.3 %cluster_attention.1 = bf16[32,128,128]{2,1,0:T(8,128)(2,1)} custom-call(bf16[32,384,128]{2,1,0:T(8,128)(2,1)S(1)} %all-to-all-done.got_ref), custom_call_target="tpu_custom_call" | custom-call | flops 8589934592 | bytes 4194304 | tf_op jit(solution)/shard_map/cluster_attention/pallas_call | solution.py:280
  65.7 6.6 %all-to-all-start.1 = ((bf16[32,128,128]{2,1,0:T(8,128)(2,1)}), bf16[32,128,128]{2,1,0:T(8,128)(2,1)S(1)}, u32[]{:S(2)}, u32[]{:S(2)}) async-start(bf16[32,128,128]{2,1,0:T(8,128)(2,1)} %cluster_attention.1), calls=%async_computation.1 | async-start | bytes 2097152 | tf_op jit(solution)/shard_map/all_to_all | solution.py:410
  72.4 0.5 picks.1.pick_ref
  72.9 0.0 collective-permute-done.far_ref
  72.9 1.1 %broadcast_select_fusion = bf16[2,1024,128]{2,1,0:T(8,128)(2,1)S(1)} fusion(bf16[2,1024,128]{2,1,0:T(8,128)(2,1)} %collective-permute-done.far_ref, bf16[2,1024,128]{2,1,0:T(8,128)(2,1)} %pad_maximum_fusion, pred[]{:T(512)S(6)} %eq.5), kind=kLoop, calls=%fused_computation.1 | loop fusion | flops 262144 | bytes 1572865 | tf_op jit(solution)/shard_map/jit(_where)/select_n | solution.py:411
  74.0 0.5 collective-permute-start.1
  74.5 1.7 %collective-permute-done.1.near_ref = bf16[2,1024,128]{2,1,0:T(8,128)(2,1)S(1)} collective-permute-done((bf16[2,1024,128]{2,1,0:T(8,128)(2,1)S(1)}, bf16[2,1024,128]{2,1,0:T(8,128)(2,1)S(1)}, u32[]{:S(2)}, u32[]{:S(2)}) %collective-permute-start.1) | collective-permute-done | bytes 524320 | tf_op jit(solution)/shard_map/ppermute | solution.py:412
  76.2 0.0 copy-start.1
  76.2 0.9 %copy-done.1 = bf16[1,1024,128]{2,1,0:T(8,128)(2,1)S(1)} copy-done((bf16[1,1024,128]{2,1,0:T(8,128)(2,1)S(1)}, bf16[1,1024,128]{2,1,0:T(8,128)(2,1)}, u32[]{:S(2)}) %copy-start.1) | copy-done | bytes 262168
  77.2 0.0 copy-start.2
  77.2 0.9 %copy-done.2 = bf16[1,1024,128]{2,1,0:T(8,128)(2,1)S(1)} copy-done((bf16[1,1024,128]{2,1,0:T(8,128)(2,1)S(1)}, bf16[1,1024,128]{2,1,0:T(8,128)(2,1)}, u32[]{:S(2)}) %copy-start.2) | copy-done | bytes 262168
  78.1 5.1 %window_attention.1 = bf16[1024,128]{1,0:T(8,128)(2,1)} custom-call(s32[1]{0:T(128)} %bitcast.4.at_ref, bf16[1024,128]{1,0:T(8,128)(2,1)S(1)} %bitcast.12, bf16[1024,128]{1,0:T(8,128)(2,1)S(1)} %bitcast.10, bf16[1024,128]{1,0:T(8,128)(2,1)S(1)} %bitcast.11, bf16[2,1024,128]{2,1,0:T(8,128)(2,1)} %collective-permute-done.far_ref, ...), custom_call_target="tpu_custom_call" | custom-call | flops 1207959552 | bytes 2097152 | tf_op jit(solution)/shard_map/window_attention/pallas_call | solution.py:336
  83.3 6.0 %all-to-all-done.1.back_ref = bf16[32,128,128]{2,1,0:T(8,128)(2,1)S(1)} async-done(((bf16[32,128,128]{2,1,0:T(8,128)(2,1)}), bf16[32,128,128]{2,1,0:T(8,128)(2,1)S(1)}, u32[]{:S(2)}, u32[]{:S(2)}) %all-to-all-start.1) | async-done | bytes 1048608 | tf_op jit(solution)/shard_map/all_to_all | solution.py:410
  89.2 2.1 %unpack_slots.1 = bf16[1024,128]{1,0:T(8,128)(2,1)} custom-call(s32[8,128]{1,0:T(8,128)S(1)} %get-tuple-element.13.start_ref, bf16[1024,1024]{1,0:T(8,128)(2,1)S(1)} %picks.1.pick_ref, bf16[32,128,128]{2,1,0:T(8,128)(2,1)S(1)} %all-to-all-done.1.back_ref), custom_call_target="tpu_custom_call" | custom-call | tf_op jit(solution)/shard_map/unpack_slots/pallas_call | solution.py:382
Async XLA Ops:
  5.3 8.8 %copy-start = (bf16[1,1024,128]{2,1,0:T(8,128)(2,1)S(1)}, bf16[1,1024,128]{2,1,0:T(8,128)(2,1)}, u32[]{:S(2)}) copy-start(bf16[1,1024,128]{2,1,0:T(8,128)(2,1)} %param.12) | copy-start | bytes 786436
  5.3 48.5 %all-to-all-start = ((bf16[32,384,128]{2,1,0:T(8,128)(2,1)}), bf16[32,384,128]{2,1,0:T(8,128)(2,1)S(1)}, u32[]{:S(2)}, u32[]{:S(2)}) async-start(bf16[32,384,128]{2,1,0:T(8,128)(2,1)} %get-tuple-element.14), calls=%async_computation | async-start | bytes 6291456 | tf_op jit(solution)/shard_map/all_to_all | solution.py:402
  53.8 19.1 %collective-permute-start = (bf16[2,1024,128]{2,1,0:T(8,128)(2,1)}, bf16[2,1024,128]{2,1,0:T(8,128)(2,1)}, u32[]{:S(2)}, u32[]{:S(2)}) collective-permute-start(bf16[2,1024,128]{2,1,0:T(8,128)(2,1)} %pad_maximum_fusion), channel_id=1, source_target_pairs={{0,2},{1,3},{2,4},{3,5},{4,6},{5,7},{6,8},{7,9},{8,10},{9,11},{10,... | collective-permute-start | bytes 1572872 | tf_op jit(solution)/shard_map/ppermute | solution.py:395
  65.7 23.5 %all-to-all-start.1 = ((bf16[32,128,128]{2,1,0:T(8,128)(2,1)}), bf16[32,128,128]{2,1,0:T(8,128)(2,1)S(1)}, u32[]{:S(2)}, u32[]{:S(2)}) async-start(bf16[32,128,128]{2,1,0:T(8,128)(2,1)} %cluster_attention.1), calls=%async_computation.1 | async-start | bytes 2097152 | tf_op jit(solution)/shard_map/all_to_all | solution.py:410
  74.0 2.2 %collective-permute-start.1 = (bf16[2,1024,128]{2,1,0:T(8,128)(2,1)S(1)}, bf16[2,1024,128]{2,1,0:T(8,128)(2,1)S(1)}, u32[]{:S(2)}, u32[]{:S(2)}) collective-permute-start(bf16[2,1024,128]{2,1,0:T(8,128)(2,1)S(1)} %broadcast_select_fusion), channel_id=1, source_target_pairs={{0,1},{1,0},{2,3},{3,2},{4,5},{5,4},{6,7},{7,6},{8,9},{9,8},{10,11... | collective-permute-start | bytes 1572872 | tf_op jit(solution)/shard_map/ppermute | solution.py:412
  76.2 1.0 %copy-start.1 = (bf16[1,1024,128]{2,1,0:T(8,128)(2,1)S(1)}, bf16[1,1024,128]{2,1,0:T(8,128)(2,1)}, u32[]{:S(2)}) copy-start(bf16[1,1024,128]{2,1,0:T(8,128)(2,1)} %param.13) | copy-start | bytes 786436
  77.2 0.9 %copy-start.2 = (bf16[1,1024,128]{2,1,0:T(8,128)(2,1)S(1)}, bf16[1,1024,128]{2,1,0:T(8,128)(2,1)}, u32[]{:S(2)}) copy-start(bf16[1,1024,128]{2,1,0:T(8,128)(2,1)} %param.11) | copy-start | bytes 786436
